TPU v7x, 32 devices: a whole 2x2x4 slice. The times are simulated.
32 devices in a mesh: row: 4 (over y, x), col: 2 (over core), expert: 4 (over z).
Axes of the slice: x: 2, y: 2, z: 4, core: 2. Of those that a mesh axis runs over, the one named last changes fastest.
Arguments:
- tokens: bfloat16 [16384, 1024], P(('row', 'col', 'expert')), may hold values from -6 to 6
- query_weight: bfloat16 [1024, 1024], P('row', 'col'), may hold values from -0.75 to 0.75
- key_projection: bfloat16 [1024, 512], P('row', 'col'), may hold values from -0.75 to 0.75
- value_projection: bfloat16 [1024, 512], P('row', 'col'), may hold values from -0.1875 to 0.1875
- output_weight: bfloat16 [1024, 1024], P('row', 'col'), may hold values from -3 to 3
- router_weight: bfloat16 [1024, 32], P('row', 'col'), may hold values from -0.09375 to 0.09375
- attention_gain: bfloat16 [1024], P(('row', 'col')), may hold values from 0.5 to 1.5
- mixture_gain: bfloat16 [1024], P(('row', 'col')), may hold values from 0.5 to 1.5
- gate_weight: bfloat16 [1024, 32, 512], P(('row', 'col'), 'expert'), may hold values from -0.375 to 0.375
- up_weight: bfloat16 [1024, 32, 512], P(('row', 'col'), 'expert'), may hold values from -0.375 to 0.375
- down_weight: bfloat16 [1024, 32, 512], P(('row', 'col'), 'expert'), may hold values from -1 to 1
- choices: int32 [16384, 8], P(('row', 'col', 'expert')), may hold values from 0 to 31, all different within a row; in each aligned block of 512 rows (0 to 511, 512 to 1023, ...) at most 144 rows name the same one
- cotangent: bfloat16 [16384, 1024], P(('row', 'col', 'expert')), may hold values from -6 to 6
Outputs:
- layer_output: bfloat16 [16384, 1024], P(('row', 'col', 'expert'))
- input_gradient: float32 [16384, 1024], P(('row', 'col', 'expert'))
- query_gradient: float32 [1024, 1024], P('row', 'col')
- key_gradient: float32 [1024, 512], P('row', 'col')
- value_gradient: float32 [1024, 512], P('row', 'col')
- output_gradient: float32 [1024, 1024], P('row', 'col')
- router_gradient: float32 [1024, 32], P('row', 'col')
- attention_gradient: float32 [1024], P(('row', 'col'))
- mixture_gradient: float32 [1024], P(('row', 'col'))
- gate_gradient: float32 [1024, 32, 512], P(('row', 'col'), 'expert')
- up_gradient: float32 [1024, 32, 512], P(('row', 'col'), 'expert')
- down_gradient: float32 [1024, 32, 512], P(('row', 'col'), 'expert')
Inputs may be any that keep to these rules, and one draw needn't show every extreme that they name: `choices`: in the rows of one device each token names 8 different experts, no expert is named by more than 144 rows, a bound that some block reaches.
All inputs are finite; a program needn't handle non-finite values.
Results may differ from a plain program's by a relative error of at most 0.02.
Values may be sent and summed in bfloat16 or wider, within the bound.
A program may use at most 256 MiB of HBM per device.

v0:
```python
import jax
import jax.numpy as jnp
from jax import lax
from jax.sharding import PartitionSpec as P

QUERY_HEADS = 16
KEY_VALUE_HEADS = 8
HEAD_SIZE = 64
EXPERTS = 32
TOP = 8
MOST = 144


score_factor = 0.015625
branch_factor = 0.22
norm_epsilon = 1e-06
rotary_base = 10000.0
masked_score = -1e30


def root_norm(values, gain_row):
    return (
        values
        * lax.rsqrt(jnp.mean(values * values, axis=-1, keepdims=True) + norm_epsilon)
        * gain_row
    )


def rotary_tables(sequence_length):
    half_width = HEAD_SIZE // 2
    inverse = rotary_base ** (-(jnp.arange(half_width, dtype=jnp.float32) * 2.0 / HEAD_SIZE))
    angles = jnp.arange(sequence_length, dtype=jnp.float32)[:, None] * inverse[None, :]
    cosine_values = jnp.concatenate([jnp.cos(angles), jnp.cos(angles)], axis=1)
    sine_values = jnp.concatenate([jnp.sin(angles), jnp.sin(angles)], axis=1)
    return (cosine_values, sine_values)


def apply_rotation(values, cosine_values, sine_values):
    half_width = values.shape[-1] // 2
    turned = jnp.concatenate([-values[..., half_width:], values[..., :half_width]], axis=-1)
    return values * cosine_values + turned * sine_values


def unrotate(incoming, cosine_values, sine_values):
    half_width = incoming.shape[-1] // 2
    scaled = incoming * sine_values
    turned = jnp.concatenate([scaled[..., half_width:], -scaled[..., :half_width]], axis=-1)
    return incoming * cosine_values + turned


def slot_tables(choice_rows):
    flat_ids = choice_rows.reshape(-1)
    count_all = flat_ids.shape[0]
    one_hot = (flat_ids[:, None] == jnp.arange(EXPERTS, dtype=jnp.int32)[None, :]).astype(jnp.int32)
    earlier = jnp.cumsum(one_hot, axis=0) - one_hot
    slot_rank = jnp.sum(earlier * one_hot, axis=1)
    slot_index = flat_ids * MOST + slot_rank
    assign_of = (
        jnp.zeros((EXPERTS * MOST,), jnp.int32)
        .at[slot_index]
        .set(jnp.arange(count_all, dtype=jnp.int32))
    )
    filled = jnp.zeros((EXPERTS * MOST,), jnp.int32).at[slot_index].set(1)
    return (slot_index, assign_of, filled)


def query_heads(input_rows, query_groups):
    return input_rows.reshape(
        input_rows.shape[0], KEY_VALUE_HEADS, query_groups, HEAD_SIZE
    ).transpose(1, 2, 0, 3)


def shared_heads(input_rows):
    return input_rows.reshape(input_rows.shape[0], KEY_VALUE_HEADS, HEAD_SIZE).transpose(1, 0, 2)


def joined_query(heads):
    return heads.transpose(2, 0, 1, 3).reshape(heads.shape[2], -1)


def joined_shared(heads):
    return heads.transpose(1, 0, 2).reshape(heads.shape[1], -1)


def block_scores(query_block, key_rotated, begin_row, end_row):
    block_rows = end_row - begin_row
    scores = (
        jnp.einsum("gqd,kd->gqk", query_block, key_rotated, preferred_element_type=jnp.float32)
        * score_factor
    )
    causal = begin_row + jnp.arange(block_rows)[:, None] >= jnp.arange(end_row)[None, :]
    return jnp.where(causal, scores, masked_score)


def head_forward(operands):
    query_rotated, key_rotated, value_low = operands
    sequence_length = key_rotated.shape[0]
    block_rows = min(512, sequence_length)
    scores = block_scores(query_rotated, key_rotated, 0, block_rows)
    row_max = jnp.max(scores, axis=-1, keepdims=True)
    log_total = row_max + jnp.log(jnp.sum(jnp.exp(scores - row_max), axis=-1, keepdims=True))
    weights_low = jnp.exp(scores - log_total).astype(jnp.bfloat16)
    mixed_parts = [
        jnp.einsum("gqk,kd->gqd", weights_low, value_low, preferred_element_type=jnp.float32)
    ]
    total_parts = [log_total]
    return (jnp.concatenate(mixed_parts, axis=1), jnp.concatenate(total_parts, axis=1))


def head_backward(operands):
    query_rotated, key_rotated, value_low, mixed_grad, log_totals = operands
    sequence_length = key_rotated.shape[0]
    block_rows = min(512, sequence_length)
    key_grad = jnp.zeros((sequence_length, HEAD_SIZE), jnp.float32)
    value_grad = jnp.zeros((sequence_length, HEAD_SIZE), jnp.float32)
    grad_block = mixed_grad[:, 0:block_rows]
    scores = block_scores(query_rotated, key_rotated, 0, block_rows)
    weights_full = jnp.exp(scores - log_totals[:, 0:block_rows])
    weight_grad = jnp.einsum(
        "gqd,kd->gqk", grad_block, value_low, preferred_element_type=jnp.float32
    )
    spread = jnp.sum(weights_full * weight_grad, axis=-1, keepdims=True)
    score_grad = (weights_full * (weight_grad - spread)).astype(jnp.bfloat16)
    query_parts = [
        jnp.einsum("gqk,kd->gqd", score_grad, key_rotated, preferred_element_type=jnp.float32)
        * score_factor
    ]
    key_grad = key_grad.at[:block_rows].add(
        jnp.einsum("gqk,gqd->kd", score_grad, query_rotated, preferred_element_type=jnp.float32)
        * score_factor
    )
    value_grad = value_grad.at[:block_rows].add(
        jnp.einsum(
            "gqk,gqd->kd",
            weights_full.astype(jnp.bfloat16),
            grad_block,
            preferred_element_type=jnp.float32,
        )
    )
    return (jnp.concatenate(query_parts, axis=1), key_grad, value_grad)


def shards(
    tokens,
    query_weight,
    key_projection,
    value_projection,
    output_weight,
    router_weight,
    attention_gain,
    mixture_gain,
    gate_weight,
    up_weight,
    down_weight,
    choices,
    cotangent,
):
    query_cols, key_cols, value_cols, output_cols, router_cols, attention_part, mixture_part = (
        lax.all_gather(query_weight, "col", axis=1, tiled=True),
        lax.all_gather(key_projection, "col", axis=1, tiled=True),
        lax.all_gather(value_projection, "col", axis=1, tiled=True),
        lax.all_gather(output_weight, "col", axis=1, tiled=True),
        lax.all_gather(router_weight, "col", axis=1, tiled=True),
        lax.all_gather(attention_gain, "col", axis=0, tiled=True),
        lax.all_gather(mixture_gain, "col", axis=0, tiled=True),
    )
    query_full, key_full, value_full, output_full, router_full, attention_full, mixture_full = (
        lax.all_gather(query_cols, "row", axis=0, tiled=True),
        lax.all_gather(key_cols, "row", axis=0, tiled=True),
        lax.all_gather(value_cols, "row", axis=0, tiled=True),
        lax.all_gather(output_cols, "row", axis=0, tiled=True),
        lax.all_gather(router_cols, "row", axis=0, tiled=True),
        lax.all_gather(attention_part, "row", axis=0, tiled=True),
        lax.all_gather(mixture_part, "row", axis=0, tiled=True),
    )
    sequence_length = tokens.shape[0]
    query_groups = QUERY_HEADS // KEY_VALUE_HEADS
    cosine_values, sine_values = rotary_tables(sequence_length)
    inputs = tokens.astype(jnp.float32)
    normed_full, first_pull = jax.vjp(root_norm, inputs, attention_full.astype(jnp.float32))
    normed = normed_full.astype(jnp.bfloat16)
    query_matrix = jnp.dot(normed, query_full, preferred_element_type=jnp.float32)
    key_matrix = jnp.dot(normed, key_full, preferred_element_type=jnp.float32)
    value_low = jnp.dot(normed, value_full, preferred_element_type=jnp.float32).astype(jnp.bfloat16)
    query_rotated = apply_rotation(
        query_heads(query_matrix, query_groups), cosine_values, sine_values
    ).astype(jnp.bfloat16)
    key_rotated = apply_rotation(shared_heads(key_matrix), cosine_values, sine_values).astype(
        jnp.bfloat16
    )
    value_head_rows = shared_heads(value_low)
    mixed_heads, log_totals = lax.map(head_forward, (query_rotated, key_rotated, value_head_rows))
    mixed_low = joined_query(mixed_heads).astype(jnp.bfloat16)
    branch = jnp.dot(mixed_low, output_full, preferred_element_type=jnp.float32)
    middle = inputs + branch_factor * branch
    second_full, second_pull = jax.vjp(root_norm, middle, mixture_full.astype(jnp.float32))
    second = second_full.astype(jnp.bfloat16)
    logits = jnp.dot(second, router_full, preferred_element_type=jnp.float32)
    pick_table = (
        choices[:, :, None] == jnp.arange(EXPERTS, dtype=jnp.int32)[None, None, :]
    ).astype(jnp.float32)
    chosen = jnp.sum(pick_table * logits[:, None, :], axis=2)
    router_gates = jax.nn.softmax(chosen, axis=1)
    slot_index, assign_of, filled = slot_tables(choices)
    live = (filled > 0)[:, None]
    send_rows = jnp.where(live, second[assign_of // TOP], jnp.zeros((), jnp.bfloat16)).reshape(
        EXPERTS, MOST, -1
    )
    arrived_rows = lax.all_to_all(send_rows, "expert", split_axis=0, concat_axis=1, tiled=True)
    gate_full, up_full, down_full = (
        lax.all_gather(gate_weight, ("row", "col"), axis=0, tiled=True),
        lax.all_gather(up_weight, ("row", "col"), axis=0, tiled=True),
        lax.all_gather(down_weight, ("row", "col"), axis=0, tiled=True),
    )
    gate_pre = jnp.einsum(
        "ecd,def->ecf", arrived_rows, gate_full, preferred_element_type=jnp.float32
    )
    up_pre = jnp.einsum("ecd,def->ecf", arrived_rows, up_full, preferred_element_type=jnp.float32)
    activated = (jax.nn.silu(gate_pre) * up_pre).astype(jnp.bfloat16)
    expert_out = jnp.einsum(
        "ecf,def->ecd", activated, down_full, preferred_element_type=jnp.float32
    ).astype(jnp.bfloat16)
    returned = lax.all_to_all(
        expert_out, "expert", split_axis=1, concat_axis=0, tiled=True
    ).reshape(EXPERTS * MOST, -1)
    picked_rows = returned[slot_index].reshape(sequence_length, TOP, -1)
    combined = jnp.sum(router_gates[:, :, None] * picked_rows, axis=1)
    layer_output = (middle + branch_factor * combined).astype(jnp.bfloat16)
    out_grad = cotangent.astype(jnp.float32)
    combined_grad = branch_factor * out_grad
    gate_grads = jnp.sum(picked_rows * combined_grad[:, None, :], axis=2)
    row_grads = (
        (router_gates[:, :, None] * combined_grad[:, None, :])
        .astype(jnp.bfloat16)
        .reshape(sequence_length * TOP, -1)
    )
    send_grads = jnp.where(live, row_grads[assign_of], jnp.zeros((), jnp.bfloat16)).reshape(
        EXPERTS, MOST, -1
    )
    arrived_grads = lax.all_to_all(send_grads, "expert", split_axis=0, concat_axis=1, tiled=True)
    gate_back, up_back, down_back = (
        lax.all_gather(gate_weight, ("row", "col"), axis=0, tiled=True),
        lax.all_gather(up_weight, ("row", "col"), axis=0, tiled=True),
        lax.all_gather(down_weight, ("row", "col"), axis=0, tiled=True),
    )
    act_grad = jnp.einsum(
        "ecd,def->ecf", arrived_grads, down_back, preferred_element_type=jnp.float32
    )
    gate_sigmoid = jax.nn.sigmoid(gate_pre)
    gate_low = (act_grad * up_pre * gate_sigmoid * (1.0 + gate_pre * (1.0 - gate_sigmoid))).astype(
        jnp.bfloat16
    )
    up_low = (act_grad * gate_pre * gate_sigmoid).astype(jnp.bfloat16)
    input_grads = jnp.einsum(
        "ecf,def->ecd", gate_low, gate_back, preferred_element_type=jnp.float32
    )
    input_grads = (
        input_grads
        + jnp.einsum("ecf,def->ecd", up_low, up_back, preferred_element_type=jnp.float32)
    ).astype(jnp.bfloat16)
    returned_grads = lax.all_to_all(
        input_grads, "expert", split_axis=1, concat_axis=0, tiled=True
    ).reshape(EXPERTS * MOST, -1)
    row_count = gate_weight.shape[0] * lax.axis_size(("row", "col"))
    rows_part = lax.slice_in_dim(arrived_rows, 0, row_count, axis=2)
    grads_part = lax.slice_in_dim(arrived_grads, 0, row_count, axis=2)
    gate_term = jnp.einsum("ecd,ecf->def", rows_part, gate_low, preferred_element_type=jnp.float32)
    up_term = jnp.einsum("ecd,ecf->def", rows_part, up_low, preferred_element_type=jnp.float32)
    down_term = jnp.einsum(
        "ecd,ecf->def", grads_part, activated, preferred_element_type=jnp.float32
    )
    expert_sums = lax.psum_scatter(
        jnp.stack([gate_term, up_term, down_term], axis=1).astype(jnp.bfloat16),
        ("row", "col"),
        scatter_dimension=0,
        tiled=True,
    ).astype(jnp.float32)
    mean_grad = jnp.sum(router_gates * gate_grads, axis=1, keepdims=True)
    chosen_grad = router_gates * (gate_grads - mean_grad)
    logit_grad = jnp.sum(pick_table * chosen_grad[:, :, None], axis=1).astype(jnp.bfloat16)
    router_part = jnp.einsum("td,te->de", second, logit_grad, preferred_element_type=jnp.float32)
    second_grad = jnp.sum(
        returned_grads[slot_index].reshape(sequence_length, TOP, -1), axis=1, dtype=jnp.float32
    )
    second_grad = second_grad + jnp.einsum(
        "te,de->td", logit_grad, router_full, preferred_element_type=jnp.float32
    )
    middle_norm_grad, mixture_grad_part = second_pull(second_grad)
    middle_grad = out_grad + middle_norm_grad
    branch_grad = (branch_factor * middle_grad).astype(jnp.bfloat16)
    output_part = jnp.einsum(
        "tf,td->fd", mixed_low, branch_grad, preferred_element_type=jnp.float32
    )
    mixed_grad = jnp.einsum(
        "td,fd->tf", branch_grad, output_full, preferred_element_type=jnp.float32
    ).astype(jnp.bfloat16)
    query_rot_grad, key_rot_grad, value_head_grad = lax.map(
        head_backward,
        (
            query_rotated,
            key_rotated,
            value_head_rows,
            query_heads(mixed_grad, query_groups),
            log_totals,
        ),
    )
    query_grad = joined_query(unrotate(query_rot_grad, cosine_values, sine_values)).astype(
        jnp.bfloat16
    )
    key_grad = joined_shared(unrotate(key_rot_grad, cosine_values, sine_values)).astype(
        jnp.bfloat16
    )
    value_grad = joined_shared(value_head_grad).astype(jnp.bfloat16)
    query_part = jnp.einsum("td,tf->df", normed, query_grad, preferred_element_type=jnp.float32)
    key_part = jnp.einsum("td,tf->df", normed, key_grad, preferred_element_type=jnp.float32)
    value_part = jnp.einsum("td,tf->df", normed, value_grad, preferred_element_type=jnp.float32)
    normed_grad = jnp.einsum(
        "tf,df->td", query_grad, query_full, preferred_element_type=jnp.float32
    )
    normed_grad = normed_grad + jnp.einsum(
        "tf,df->td", key_grad, key_full, preferred_element_type=jnp.float32
    )
    normed_grad = normed_grad + jnp.einsum(
        "tf,df->td", value_grad, value_full, preferred_element_type=jnp.float32
    )
    input_norm_grad, attention_grad_part = first_pull(normed_grad)
    input_gradient = middle_grad + input_norm_grad
    rows_query, rows_key, rows_value, rows_output, rows_router, rows_attention, rows_mixture = (
        lax.psum_scatter(
            query_part.astype(jnp.bfloat16), "row", scatter_dimension=0, tiled=True
        ).astype(jnp.float32),
        lax.psum_scatter(
            key_part.astype(jnp.bfloat16), "row", scatter_dimension=0, tiled=True
        ).astype(jnp.float32),
        lax.psum_scatter(
            value_part.astype(jnp.bfloat16), "row", scatter_dimension=0, tiled=True
        ).astype(jnp.float32),
        lax.psum_scatter(
            output_part.astype(jnp.bfloat16), "row", scatter_dimension=0, tiled=True
        ).astype(jnp.float32),
        lax.psum_scatter(
            router_part.astype(jnp.bfloat16), "row", scatter_dimension=0, tiled=True
        ).astype(jnp.float32),
        lax.psum_scatter(
            attention_grad_part.astype(jnp.bfloat16), "row", scatter_dimension=0, tiled=True
        ).astype(jnp.float32),
        lax.psum_scatter(
            mixture_grad_part.astype(jnp.bfloat16), "row", scatter_dimension=0, tiled=True
        ).astype(jnp.float32),
    )
    cols_query, cols_key, cols_value, cols_output, cols_router, cols_attention, cols_mixture = (
        lax.psum_scatter(
            rows_query.astype(jnp.bfloat16), "col", scatter_dimension=1, tiled=True
        ).astype(jnp.float32),
        lax.psum_scatter(
            rows_key.astype(jnp.bfloat16), "col", scatter_dimension=1, tiled=True
        ).astype(jnp.float32),
        lax.psum_scatter(
            rows_value.astype(jnp.bfloat16), "col", scatter_dimension=1, tiled=True
        ).astype(jnp.float32),
        lax.psum_scatter(
            rows_output.astype(jnp.bfloat16), "col", scatter_dimension=1, tiled=True
        ).astype(jnp.float32),
        lax.psum_scatter(
            rows_router.astype(jnp.bfloat16), "col", scatter_dimension=1, tiled=True
        ).astype(jnp.float32),
        lax.psum_scatter(
            rows_attention.astype(jnp.bfloat16), "col", scatter_dimension=0, tiled=True
        ).astype(jnp.float32),
        lax.psum_scatter(
            rows_mixture.astype(jnp.bfloat16), "col", scatter_dimension=0, tiled=True
        ).astype(jnp.float32),
    )
    (
        query_gradient,
        key_gradient,
        value_gradient,
        output_gradient,
        router_gradient,
        attention_gradient,
        mixture_gradient,
    ) = (
        lax.psum(cols_query.astype(jnp.bfloat16), "expert").astype(jnp.float32),
        lax.psum(cols_key.astype(jnp.bfloat16), "expert").astype(jnp.float32),
        lax.psum(cols_value.astype(jnp.bfloat16), "expert").astype(jnp.float32),
        lax.psum(cols_output.astype(jnp.bfloat16), "expert").astype(jnp.float32),
        lax.psum(cols_router.astype(jnp.bfloat16), "expert").astype(jnp.float32),
        lax.psum(cols_attention.astype(jnp.bfloat16), "expert").astype(jnp.float32),
        lax.psum(cols_mixture.astype(jnp.bfloat16), "expert").astype(jnp.float32),
    )
    return (
        layer_output,
        input_gradient,
        query_gradient,
        key_gradient,
        value_gradient,
        output_gradient,
        router_gradient,
        attention_gradient,
        mixture_gradient,
        expert_sums[:, 0],
        expert_sums[:, 1],
        expert_sums[:, 2],
    )


def solution(mesh):
    placed = (
        P(("row", "col", "expert"), None),
        P("row", "col"),
        P("row", "col"),
        P("row", "col"),
        P("row", "col"),
        P("row", "col"),
        P(("row", "col")),
        P(("row", "col")),
        P(("row", "col"), "expert", None),
        P(("row", "col"), "expert", None),
        P(("row", "col"), "expert", None),
        P(("row", "col", "expert"), None),
        P(("row", "col", "expert"), None),
    )
    return jax.shard_map(
        shards,
        mesh=mesh,
        in_specs=placed,
        out_specs=(
            P(("row", "col", "expert"), None),
            P(("row", "col", "expert"), None),
            P("row", "col"),
            P("row", "col"),
            P("row", "col"),
            P("row", "col"),
            P("row", "col"),
            P(("row", "col")),
            P(("row", "col")),
            P(("row", "col"), "expert", None),
            P(("row", "col"), "expert", None),
            P(("row", "col"), "expert", None),
        ),
        check_vma=False,
    )
```

profile of v0, /device:TPU:0, one launch (start us, length us, event | category | flops | bytes accessed | tf_op | source)
XLA Modules:
  0.0 1747.8 jit_solution(1814157840320317318)
XLA Ops:
  64.3 18.1 %reduce-window.6 = s32[32,32,128]{2,1,0:T(8,128)} reduce-window(s32[32,32,128]{2,1,0:T(8,128)} %fusion.56, s32[]{:T(128)} %copy.175), window={size=1x1x128 pad=0_0x0_0x127_0}, to_apply=%region_9.10 | reduce-window | flops 16646144 | bytes 1048580 | tf_op jit(solution)/shard_map/reduce-window
  86.1 15.5 scatter_custom_fusion.1
  102.3 15.8 scatter_custom_fusion
  131.7 34.8 %while.35 = (s32[]{:T(128)}, bf16[8,2,512,64]{2,3,1,0:T(8,128)(2,1)}, f32[8,2,512,1]{2,1,3,0:T(2,128)}, bf16[8,2,512,64]{2,3,1,0:T(8,128)(2,1)}, bf16[8,512,64]{1,2,0:T(8,128)(2,1)}, /*index=5*/bf16[8,512,64]{1,2,0:T(8,128)(2,1)}) while((s32[]{:T(128)}, bf16[8,2,512,64]{2,3,1,0:T(8,128)(2,1)}, f32[8,2,512,1]{2,1,3,0:T(2,128)}, ...), condition=%wide.region_4.5_spmd.clone, body=%wide.region_1.4_spmd.sunk.clone | while | flops 138148864 | bytes 7374929 | solution.py:192
  172.2 14.9 gather_fusion
  191.2 25.3 %gather_fusion.2 = bf16[4608,1024]{1,0:T(8,128)(2,1)} fusion(bf16[4096,1024]{1,0:T(8,128)(2,1)} %fusion.39, s32[5120]{0:T(1024)S(1)} %get-tuple-element.378), kind=kCustom, calls=%fused_computation.2 | custom fusion | bytes 18892800 | tf_op jit(solution)/shard_map/gather | solution.py:237
  216.5 14.0 broadcast_select_fusion
  237.8 202.8 %all-to-all-done = bf16[32,144,1024]{2,1,0:T(8,128)(2,1)} async-done(((bf16[32,144,1024]{2,1,0:T(8,128)(2,1)}), bf16[32,144,1024]{2,1,0:T(8,128)(2,1)}, u32[]{:S(2)}, u32[]{:S(2)}) %all-to-all-start) | async-done | bytes 9437216 | tf_op jit(solution)/shard_map/all_to_all | solution.py:209
  457.1 194.4 %all-to-all-done.2 = bf16[32,144,1024]{2,1,0:T(8,128)(2,1)} async-done(((bf16[32,144,1024]{2,1,0:T(8,128)(2,1)}), bf16[32,144,1024]{2,1,0:T(8,128)(2,1)}, u32[]{:S(2)}, u32[]{:S(2)}) %all-to-all-start.2) | async-done | bytes 9437216 | tf_op jit(solution)/shard_map/all_to_all | solution.py:240
  685.4 18.5 %multiply_convert_fusion.1 = (bf16[8,576,512]{2,1,0:T(8,128)(2,1)}, bf16[8,576,512]{2,1,0:T(8,128)(2,1)}, bf16[8,576,512]{2,1,0:T(8,128)(2,1)}) fusion(f32[8,576,512]{2,1,0:T(8,128)} %fusion.85, f32[8,576,512]{2,1,0:T(8,128)} %fusion.86, bf16[8,576,1024]{2,1,0:T(8,128)(2,1)} %bitcast.279, bf16[1024,8,512]{2,0,1:T(8,128)(2,1)} %all-gather.24.cloned.1.call-done), kind=kOutput, calls=%fused_computation.67 | convolution fusion | flops 4869586944 | bytes 50855936 | tf_op jit(solution)/shard_map/ecd,def->ecf/dot_general | solution.py:246
  716.6 17.0 add_convert_fusion
  775.8 181.2 %all-to-all-done.3 = bf16[8,576,1024]{2,0,1:T(8,128)(2,1)} async-done(((bf16[8,576,1024]{2,0,1:T(8,128)(2,1)}), bf16[8,576,1024]{2,0,1:T(8,128)(2,1)}, u32[]{:S(2)}, u32[]{:S(2)}) %all-to-all-start.3) | async-done | bytes 9437216 | tf_op jit(solution)/shard_map/all_to_all | solution.py:261
  975.9 26.1 %gather_fusion.3 = bf16[4096,1024]{1,0:T(8,128)(2,1)} fusion(bf16[4608,1024]{1,0:T(8,128)(2,1)} %bitcast.270, s32[4096]{0:T(1024)S(1)} %broadcast_clamp_fusion), kind=kCustom, calls=%fused_computation.3 | custom fusion | bytes 16793600 | tf_op jit(solution)/shard_map/gather | solution.py:283
  1013.9 154.1 %all-to-all-done.1 = bf16[8,576,1024]{2,0,1:T(8,128)(2,1)} async-done(((bf16[8,576,1024]{2,0,1:T(8,128)(2,1)}), bf16[8,576,1024]{2,0,1:T(8,128)(2,1)}, u32[]{:S(2)}, u32[]{:S(2)}) %all-to-all-start.1) | async-done | bytes 9437216 | tf_op jit(solution)/shard_map/all_to_all | solution.py:223
  1180.7 25.9 %gather_fusion.1 = bf16[4096,1024]{1,0:T(8,128)(2,1)} fusion(bf16[4608,1024]{1,0:T(8,128)(2,1)} %bitcast.269, s32[4096]{0:T(1024)S(1)} %broadcast_clamp_fusion), kind=kCustom, calls=%fused_computation.1 | custom fusion | bytes 16793600 | tf_op jit(solution)/shard_map/gather | solution.py:226
  1227.0 68.7 %while.36 = (s32[]{:T(128)}, f32[8,2,512,64]{2,3,1,0:T(8,128)S(1)}, f32[8,512,64]{1,2,0:T(8,128)}, bf16[8,512,64]{1,2,0:T(8,128)(2,1)}, bf16[8,2,512,64]{2,3,1,0...) while((s32[]{:T(128)}, f32[8,2,512,64]{2,3,1,0:T(8,128)S(1)}, ...), condition=%wide.region_22.23_spmd.clone, body=%wide.region_20.22_spmd.sunk.clone | while | flops 340622336 | bytes 17523816 | solution.py:297
  1328.0 30.8 %reduce-scatter.22.cloned.1.call-done = bf16[256,512]{1,0:T(8,128)(2,1)} async-done(((bf16[1024,512]{1,0:T(8,128)(2,1)}), bf16[256,512]{1,0:T(8,128)(2,1)}) %reduce-scatter.22.cloned.1.call-update) | async-done | bytes 262160 | tf_op jit(solution)/shard_map/reduce_scatter | solution.py:335
  1358.9 38.6 %reduce-scatter.14.cloned.1.call-done = bf16[256,1024]{1,0:T(8,128)(2,1)} async-done(((bf16[1024,1024]{1,0:T(8,128)(2,1)}), bf16[256,1024]{1,0:T(8,128)(2,1)}) %reduce-scatter.14.cloned.1.call-update) | async-done | bytes 524304 | tf_op jit(solution)/shard_map/reduce_scatter | solution.py:329
  1397.5 13.3 convert_bitcast_fusion
  1410.8 25.7 %reduce-scatter.26.cloned.1.call-done = bf16[256,1024]{1,0:T(8,128)(2,1)} async-done(((bf16[1024,1024]{1,0:T(8,128)(2,1)}), bf16[256,1024]{1,0:T(8,128)(2,1)}) %reduce-scatter.26.cloned.1.call-update) | async-done | bytes 524304 | tf_op jit(solution)/shard_map/reduce_scatter | solution.py:338
  1449.9 13.5 reduce-scatter.30.cloned.1.call-done
  1506.9 17.6 %pad_maximum_fusion = bf16[1024,3,8,512]{0,3,2,1:T(8,128)(2,1)} fusion(bf16[1024,1,8,512]{0,3,2,1:T(8,128)(2,1)} %convert_bitcast_fusion, bf16[1024,1,8,512]{0,3,2,1:T(8,128)(2,1)} %convert_bitcast_fusion.1, bf16[1024,1,8,512]{0,3,2,1:T(8,128)(2,1)} %convert_bitcast_fusion.2), kind=kLoop, calls=%fused_computation.58 | loop fusion | flops 25165824 | bytes 50331648 | tf_op jit(solution)/shard_map/stack | solution.py:273
  1524.5 32.8 %copy.140 = bf16[1024,12288]{1,0:T(8,128)(2,1)} copy(bf16[1024,12288]{0,1:T(8,128)(2,1)} %bitcast.271) | data formatting | bytes 50331648
  1604.8 121.3 %reduce-scatter.34.cloned.1.call-done = bf16[128,12288]{1,0:T(8,128)(2,1)} async-done(((bf16[1024,12288]{1,0:T(8,128)(2,1)}), bf16[128,12288]{1,0:T(8,128)(2,1)}) %reduce-scatter.34.cloned.1.call-update) | async-done | bytes 3145744
  (414 shorter events, 513.6 us)
Async XLA Ops:
  7.2 113.4 %all-gather.14.cloned.1.call-start = ((), (), s32[]{:S(2)}) async-start(), calls=%async_computation.16 | async-start | bytes 1310720 | tf_op jit(solution)/shard_map/all_gather | solution.py:169
  11.3 112.6 %all-gather.16.cloned.1.call-start = ((), (), s32[]{:S(2)}) async-start(), calls=%async_computation.17 | async-start | bytes 1310720 | tf_op jit(solution)/shard_map/all_gather | solution.py:170
  15.1 111.7 %all-gather.12.cloned.1.call-start = ((), (), s32[]{:S(2)}) async-start(), calls=%async_computation.15 | async-start | bytes 2621440 | tf_op jit(solution)/shard_map/all_gather | solution.py:168
  19.2 147.3 %all-gather.18.cloned.1.call-start = ((), (), s32[]{:S(2)}) async-start(), calls=%async_computation.18 | async-start | bytes 2621440 | tf_op jit(solution)/shard_map/all_gather | solution.py:171
  21.7 638.9 %all-gather.20.cloned.1.call-start = ((), (), s32[]{:S(2)}) async-start(), calls=%async_computation.19 | async-start | bytes 9437184 | tf_op jit(solution)/shard_map/all_gather | solution.py:211
  230.5 210.0 %all-to-all-start = ((bf16[32,144,1024]{2,1,0:T(8,128)(2,1)}), bf16[32,144,1024]{2,1,0:T(8,128)(2,1)}, u32[]{:S(2)}, u32[]{:S(2)}) async-start(bf16[32,144,1024]{2,1,0:T(8,128)(2,1)} %get-tuple-element.369), calls=%async_computation | async-start | bytes 18874368 | tf_op jit(solution)/shard_map/all_to_all | solution.py:209
  236.4 436.8 %all-gather.22.cloned.1.call-start = ((), (), s32[]{:S(2)}) async-start(), calls=%async_computation.20 | async-start | bytes 9437184 | tf_op jit(solution)/shard_map/all_gather | solution.py:212
  440.6 210.9 %all-to-all-start.2 = ((bf16[32,144,1024]{2,1,0:T(8,128)(2,1)}), bf16[32,144,1024]{2,1,0:T(8,128)(2,1)}, u32[]{:S(2)}, u32[]{:S(2)}) async-start(bf16[32,144,1024]{2,1,0:T(8,128)(2,1)} %get-tuple-element.368), calls=%async_computation.2 | async-start | bytes 18874368 | tf_op jit(solution)/shard_map/all_to_all | solution.py:240
  446.5 238.9 %all-gather.24.cloned.1.call-start = ((), (), s32[]{:S(2)}) async-start(), calls=%async_computation.21 | async-start | bytes 9437184 | tf_op jit(solution)/shard_map/all_gather | solution.py:213
  746.2 210.9 %all-to-all-start.3 = ((bf16[8,576,1024]{2,0,1:T(8,128)(2,1)}), bf16[8,576,1024]{2,0,1:T(8,128)(2,1)}, u32[]{:S(2)}, u32[]{:S(2)}) async-start(bf16[8,576,1024]{2,0,1:T(8,128)(2,1)} %copy.125), calls=%async_computation.3 | async-start | bytes 18874368 | tf_op jit(solution)/shard_map/all_to_all | solution.py:261
  775.8 187.4 %copy-start.41 = (s32[4096,1]{0,1:T(1,128)S(1)}, s32[4096,1]{0,1:T(1,128)}, u32[]{:S(2)}) copy-start(s32[4096,1]{0,1:T(1,128)} %copy-done.40) | copy-start | bytes 49156
  957.0 210.9 %all-to-all-start.1 = ((bf16[8,576,1024]{2,0,1:T(8,128)(2,1)}), bf16[8,576,1024]{2,0,1:T(8,128)(2,1)}, u32[]{:S(2)}, u32[]{:S(2)}) async-start(bf16[8,576,1024]{2,0,1:T(8,128)(2,1)} %copy.121), calls=%async_computation.1 | async-start | bytes 18874368 | tf_op jit(solution)/shard_map/all_to_all | solution.py:223
  962.9 365.0 %reduce-scatter.18.cloned.1.call-start = ((), (), s32[]{:S(2)}) async-start(), calls=%async_computation.24 | async-start | bytes 1310720 | tf_op jit(solution)/shard_map/reduce_scatter | solution.py:332
  1301.7 57.1 %reduce-scatter.22.cloned.1.call-start = ((), (), s32[]{:S(2)}) async-start(), calls=%async_computation.26 | async-start | bytes 1310720 | tf_op jit(solution)/shard_map/reduce_scatter | solution.py:335
  1303.9 93.6 %reduce-scatter.14.cloned.1.call-start = ((), (), s32[]{:S(2)}) async-start(), calls=%async_computation.22 | async-start | bytes 2621440 | tf_op jit(solution)/shard_map/reduce_scatter | solution.py:329
  1311.9 124.6 %reduce-scatter.26.cloned.1.call-start = ((), (), s32[]{:S(2)}) async-start(), calls=%async_computation.28 | async-start | bytes 2621440 | tf_op jit(solution)/shard_map/reduce_scatter | solution.py:338
  1317.4 146.0 %reduce-scatter.30.cloned.1.call-start = ((), (), s32[]{:S(2)}) async-start(), calls=%async_computation.30 | async-start | bytes 81920 | tf_op jit(solution)/shard_map/reduce_scatter | solution.py:341
  1319.5 157.5 %reduce-scatter.20.cloned.1.call-start = ((), (), s32[]{:S(2)}) async-start(), calls=%async_computation.25 | async-start | bytes 393216 | tf_op jit(solution)/shard_map/reduce_scatter | solution.py:355
  1328.0 156.4 %reduce-scatter.24.cloned.1.call-start = ((), (), s32[]{:S(2)}) async-start(), calls=%async_computation.27 | async-start | bytes 393216 | tf_op jit(solution)/shard_map/reduce_scatter | solution.py:358
  1358.9 136.8 %reduce-scatter.16.cloned.1.call-start = ((), (), s32[]{:S(2)}) async-start(), calls=%async_computation.23 | async-start | bytes 786432 | tf_op jit(solution)/shard_map/reduce_scatter | solution.py:352
  1397.5 109.4 %reduce-scatter.28.cloned.1.call-start = ((), (), s32[]{:S(2)}) async-start(), calls=%async_computation.29 | async-start | bytes 786432 | tf_op jit(solution)/shard_map/reduce_scatter | solution.py:361
  1436.5 147.7 %reduce-scatter.32.cloned.1.call-start = ((), (), s32[]{:S(2)}) async-start(), calls=%async_computation.31 | async-start | bytes 24576 | tf_op jit(solution)/shard_map/reduce_scatter | solution.py:364
  1463.4 134.4 %all-reduce.10.cloned.1.call-start = ((), (), s32[]{:S(2)}) async-start(), calls=%async_computation.33 | async-start | bytes 1572864 | tf_op jit(solution)/shard_map/psum | solution.py:383
  1506.9 219.2 %reduce-scatter.34.cloned.1.call-start = ((), (), s32[]{:S(2)}) async-start(), calls=%async_computation.32 | async-start | bytes 28311552
  (64 other events, 780.8 us)
Sparse Core Ops, SparseCore 0:
  11.5 29.0 all-gather.13
  42.4 26.6 all-gather.15
  70.9 35.3 all-gather.11
  108.0 35.2 all-gather.17
  145.7 54.3 all-gather.19
  239.4 54.8 all-gather.21
  449.9 54.9 all-gather.23
  1301.8 26.0 reduce-scatter.17
  1331.1 27.7 reduce-scatter.21
  1362.2 35.1 reduce-scatter.13
  1401.3 35.1 reduce-scatter.25
  1439.7 23.6 reduce-scatter.29
  1465.7 7.6 reduce-scatter.19
  1475.5 8.7 reduce-scatter.23
  1486.5 9.1 reduce-scatter.15
  1497.7 9.0 reduce-scatter.27
  1509.0 8.5 reduce-scatter.31
  1520.2 45.8 all-reduce.9
  1570.1 155.9 reduce-scatter.33
where the time goes:
time: 1760 us; the launch traced here: 1750 us
  waiting for transfers between devices  1000 us (57%)
  local copies, waits for them, and re-layouts  269 us (15%)
  matrix products  242 us (14%)
  other arithmetic  125 us (7%)
  blocking collectives  68.7 us (4%)
  starting transfers between devices  25 us (1%)
    all_to_all x1, waiting for transfers between devices, shards(): lax.all_to_all(send_rows, 'expert', split_axis=0, concat_axis=1, tiled=True)  203 us
    all_to_all x1, waiting for transfers between devices, shards(): lax.all_to_all(send_grads, 'expert', split_axis=0, concat_axis=1, tiled=T...  194 us
    all_to_all x1, waiting for transfers between devices, shards(): lax.all_to_all(input_grads, 'expert', split_axis=1, concat_axis=0, tiled=...  181 us
    all_to_all x1, waiting for transfers between devices, shards(): lax.all_to_all(expert_out, 'expert', split_axis=1, concat_axis=0, tiled=T...  154 us
    unnamed x20, waiting for transfers between devices  122 us
    unnamed x145, local copies, waits for them, and re-layouts  61.5 us
    reduce_scatter x1, waiting for transfers between devices, shards(): lax.psum_scatter(query_part.astype(jnp.bfloat16), 'row', scatter_dimensio...  38.6 us
  transfers between devices with their start and end apart: 23, of which 13 were waited for; matrix products, arithmetic and copies ran while one was open for 24% of the time, Pallas kernels for 0%

commit v1 on v0

v1 whole, which is shorter than its diff:
```python
import functools

import jax
import jax.numpy as jnp
from jax import lax
from jax.experimental import pallas as pl
from jax.experimental.pallas import tpu as pltpu
from jax.sharding import PartitionSpec as P

HEAD_SIZE = 64
EXPERTS = 32
MOST = 144

score_factor = 0.015625
branch_factor = 0.22
norm_epsilon = 1e-06
rotary_base = 10000.0
masked_score = -1e30
bf16 = jnp.bfloat16
f32 = jnp.float32


def dot(a, b, a_dim, b_dim):
    return lax.dot_general(a, b, (((a_dim,), (b_dim,)), ((), ())), preferred_element_type=f32)


def rotary_tables(sequence_length):
    half_width = HEAD_SIZE // 2
    inverse = rotary_base ** (-(jnp.arange(half_width, dtype=f32) * 2.0 / HEAD_SIZE))
    angles = jnp.arange(sequence_length, dtype=f32)[:, None] * inverse[None, :]
    cosine, sine = jnp.cos(angles), jnp.sin(angles)
    return (
        jnp.concatenate([cosine] * 4, axis=1),
        jnp.concatenate([-sine, sine, -sine, sine], axis=1),
    )


def turned(values):
    half = HEAD_SIZE // 2
    lane = lax.broadcasted_iota(jnp.int32, values.shape, 1)
    ahead = pltpu.roll(values, values.shape[1] - half, 1)
    behind = pltpu.roll(values, half, 1)
    return jnp.where(lane % HEAD_SIZE < half, ahead, behind)


def causal_scores(query, keys, begin):
    scores = dot(query, keys, 1, 1) * score_factor
    rows = begin + lax.broadcasted_iota(jnp.int32, scores.shape, 0)
    return jnp.where(rows >= lax.broadcasted_iota(jnp.int32, scores.shape, 1), scores, masked_score)


def attention_forward(
    query_width, key_width, qkv_ref, cos_ref, sin_ref, query_ref, key_ref, value_ref, mixed_ref, log_ref
):
    length = qkv_ref.shape[1]
    block = min(256, length)
    cosine, sine = cos_ref[...], sin_ref[...]
    for start in range(0, query_width + key_width, 128):
        values = qkv_ref[0, :, start : start + 128]
        rotated = (values * cosine + turned(values) * sine).astype(bf16)
        if start < query_width:
            query_ref[0, :, start : start + 128] = rotated
        else:
            key_ref[0, :, start - query_width : start - query_width + 128] = rotated
    value_ref[0] = qkv_ref[0, :, query_width + key_width :].astype(bf16)
    groups = query_width // key_width
    lane = lax.broadcasted_iota(jnp.int32, (block, 128), 1)
    for begin in range(0, length, block):
        end = begin + block
        logs = jnp.zeros((block, 128), f32)
        for head in range(query_width // HEAD_SIZE):
            here = slice(head * HEAD_SIZE, (head + 1) * HEAD_SIZE)
            shared = slice(head // groups * HEAD_SIZE, (head // groups + 1) * HEAD_SIZE)
            scores = causal_scores(query_ref[0, begin:end, here], key_ref[0, :end, shared], begin)
            row_max = jnp.max(scores, axis=1, keepdims=True)
            weights = jnp.exp(scores - row_max)
            total = jnp.sum(weights, axis=1, keepdims=True)
            probs = (weights * (1.0 / total)).astype(bf16)
            mixed_ref[begin:end, here] = dot(probs, value_ref[0, :end, shared], 1, 0).astype(bf16)
            logs = jnp.where(lane == head, row_max + jnp.log(total), logs)
        log_ref[0, begin:end, :] = logs


def attention_backward(
    query_width,
    key_width,
    query_ref,
    key_ref,
    value_ref,
    grad_ref,
    log_ref,
    cos_ref,
    sin_ref,
    out_ref,
    dq_ref,
    dk_ref,
    dv_ref,
):
    length = query_ref.shape[1]
    block = min(256, length)
    groups = query_width // key_width
    dk_ref[...] = jnp.zeros_like(dk_ref)
    dv_ref[...] = jnp.zeros_like(dv_ref)
    for begin in range(0, length, block):
        end = begin + block
        for head in range(query_width // HEAD_SIZE):
            here = slice(head * HEAD_SIZE, (head + 1) * HEAD_SIZE)
            shared = slice(head // groups * HEAD_SIZE, (head // groups + 1) * HEAD_SIZE)
            query = query_ref[0, begin:end, here]
            keys = key_ref[0, :end, shared]
            grads = grad_ref[begin:end, here]
            scores = causal_scores(query, keys, begin)
            weights = jnp.exp(scores - log_ref[0, begin:end, head : head + 1])
            weight_grad = dot(grads, value_ref[0, :end, shared], 1, 1)
            spread = jnp.sum(weights * weight_grad, axis=1, keepdims=True)
            score_grad = (weights * (weight_grad - spread)).astype(bf16)
            dq_ref[begin:end, here] = dot(score_grad, keys, 1, 0) * score_factor
            dk_ref[:end, shared] += dot(score_grad, query, 0, 0) * score_factor
            dv_ref[:end, shared] += dot(weights.astype(bf16), grads, 0, 0)
    cosine, sine = cos_ref[...], sin_ref[...]
    for start in range(0, query_width + key_width, 128):
        if start < query_width:
            values = dq_ref[:, start : start + 128]
        else:
            values = dk_ref[:, start - query_width : start - query_width + 128]
        out_ref[0, :, start : start + 128] = (values * cosine - turned(values) * sine).astype(bf16)
    out_ref[0, :, query_width + key_width :] = dv_ref[...].astype(bf16)


def params(count):
    return pltpu.CompilerParams(
        dimension_semantics=("arbitrary",) * count, vmem_limit_bytes=56 * 1024 * 1024
    )


def run_forward(qkv, cosine, sine, query_width, key_width):
    parts, length, width = qkv.shape
    whole = lambda c: (c, 0, 0)
    table = pl.BlockSpec((length, 128), lambda c: (0, 0))
    return pl.pallas_call(
        functools.partial(attention_forward, query_width, key_width),
        grid=(parts,),
        in_specs=[pl.BlockSpec((1, length, width), whole), table, table],
        out_specs=[
            pl.BlockSpec((1, length, query_width), whole),
            pl.BlockSpec((1, length, key_width), whole),
            pl.BlockSpec((1, length, key_width), whole),
            pl.BlockSpec((length, query_width), lambda c: (0, c)),
            pl.BlockSpec((1, length, 128), whole),
        ],
        out_shape=[
            jax.ShapeDtypeStruct((parts, length, query_width), bf16),
            jax.ShapeDtypeStruct((parts, length, key_width), bf16),
            jax.ShapeDtypeStruct((parts, length, key_width), bf16),
            jax.ShapeDtypeStruct((length, parts * query_width), bf16),
            jax.ShapeDtypeStruct((parts, length, 128), f32),
        ],
        compiler_params=params(1),
        cost_estimate=pl.CostEstimate(
            flops=4 * length * length * parts * query_width,
            bytes_accessed=8 * parts * length * width,
            transcendentals=parts * length * length * query_width // HEAD_SIZE,
        ),
        name="attention_forward",
    )(qkv, cosine, sine)


def run_backward(query, key, value, grad, logs, cosine, sine):
    parts, length, query_width = query.shape
    key_width = key.shape[2]
    width = query_width + 2 * key_width
    whole = lambda c: (c, 0, 0)
    table = pl.BlockSpec((length, 128), lambda c: (0, 0))
    return pl.pallas_call(
        functools.partial(attention_backward, query_width, key_width),
        grid=(parts,),
        in_specs=[
            pl.BlockSpec((1, length, query_width), whole),
            pl.BlockSpec((1, length, key_width), whole),
            pl.BlockSpec((1, length, key_width), whole),
            pl.BlockSpec((length, query_width), lambda c: (0, c)),
            pl.BlockSpec((1, length, 128), whole),
            table,
            table,
        ],
        out_specs=pl.BlockSpec((1, length, width), whole),
        out_shape=jax.ShapeDtypeStruct((parts, length, width), bf16),
        scratch_shapes=[
            pltpu.VMEM((length, query_width), f32),
            pltpu.VMEM((length, key_width), f32),
            pltpu.VMEM((length, key_width), f32),
        ],
        compiler_params=params(1),
        cost_estimate=pl.CostEstimate(
            flops=10 * length * length * parts * query_width,
            bytes_accessed=6 * parts * length * width,
            transcendentals=parts * length * length * query_width // HEAD_SIZE,
        ),
        name="attention_backward",
    )(query, key, value, grad, logs, cosine, sine)


def dispatch_kernel(slot_ref, gate_ref, second_ref, grad_ref, rows_ref, grads_ref, gates_ref):
    expert = pl.program_id(1)
    slots = slot_ref[0, pl.ds(expert, 1), :]
    gates = gate_ref[0, pl.ds(expert, 1), :]
    match = lax.broadcasted_iota(jnp.int32, (MOST, slots.shape[1]), 0) == slots
    picks = match.astype(f32).astype(bf16)
    rows_ref[0, 0] = dot(picks, second_ref[0], 1, 0).astype(bf16)
    grads_ref[0, 0] = dot(picks, grad_ref[0], 1, 0).astype(bf16)
    gate_column = jnp.sum(jnp.where(match, gates, 0.0), axis=1, keepdims=True)
    gates_ref[0, 0] = jnp.broadcast_to(gate_column, (MOST, 128))


def run_dispatch(slots, gates, second, grad):
    sources, experts, length = slots.shape
    width = second.shape[2]
    table = pl.BlockSpec((1, experts, length), lambda s, e: (s, 0, 0))
    rows = pl.BlockSpec((1, length, width), lambda s, e: (s, 0, 0))
    out = lambda n: pl.BlockSpec((1, 1, MOST, n), lambda s, e: (e, s, 0, 0))
    return pl.pallas_call(
        dispatch_kernel,
        grid=(sources, experts),
        in_specs=[table, table, rows, rows],
        out_specs=[out(width), out(width), out(128)],
        out_shape=[
            jax.ShapeDtypeStruct((experts, sources, MOST, width), bf16),
            jax.ShapeDtypeStruct((experts, sources, MOST, width), bf16),
            jax.ShapeDtypeStruct((experts, sources, MOST, 128), f32),
        ],
        compiler_params=params(2),
        cost_estimate=pl.CostEstimate(
            flops=4 * sources * experts * MOST * length * width,
            bytes_accessed=4 * sources * experts * MOST * width,
            transcendentals=0,
        ),
        name="dispatch",
    )(slots, gates, second, grad)


def expert_kernel(rows_ref, grads_ref, gates_ref, weight_ref, out_ref, back_ref, gate_grad_ref, weight_grad_ref):
    sources, slots, width = rows_ref.shape[1:]
    count = sources * slots
    pieces, _, _, part, hidden = weight_ref.shape
    rows = rows_ref[0].reshape(count, width)
    grads = grads_ref[0].reshape(count, width)
    gates = gates_ref[0].reshape(count, 128)[:, :1] * branch_factor
    gate_weight = weight_ref[:, 0, 0].reshape(width, hidden)
    up_weight = weight_ref[:, 1, 0].reshape(width, hidden)
    down_weight = weight_ref[:, 2, 0].reshape(width, hidden)
    gate_pre = dot(rows, gate_weight, 1, 0)
    up_pre = dot(rows, up_weight, 1, 0)
    sigmoid = 1.0 / (1.0 + jnp.exp(-gate_pre))
    silu = gate_pre * sigmoid
    act = (silu * up_pre).astype(bf16).astype(f32)
    act_raw = dot(grads, down_weight, 1, 0)
    gate_grad = jnp.sum(act * act_raw, axis=1, keepdims=True) * branch_factor
    gate_grad_ref[0] = jnp.broadcast_to(gate_grad, (count, 128)).reshape(sources, slots, 128)
    scaled = (gates * act).astype(bf16)
    act_grad = gates * act_raw
    gate_low = (act_grad * up_pre * sigmoid * (1.0 + gate_pre * (1.0 - sigmoid))).astype(bf16)
    up_low = (act_grad * silu).astype(bf16)
    back = dot(gate_low, gate_weight, 1, 1) + dot(up_low, up_weight, 1, 1)
    back_ref[0] = back.astype(bf16).reshape(sources, slots, width)
    out_ref[0] = dot(scaled, down_weight, 1, 1).astype(bf16).reshape(sources, slots, width)
    shape = (pieces, part, hidden)
    weight_grad_ref[:, 0, 0] = dot(rows, gate_low, 0, 0).astype(bf16).reshape(shape)
    weight_grad_ref[:, 1, 0] = dot(rows, up_low, 0, 0).astype(bf16).reshape(shape)
    weight_grad_ref[:, 2, 0] = dot(grads, scaled, 0, 0).astype(bf16).reshape(shape)


def run_experts(rows, grads, gates, weights):
    experts, sources, slots, width = rows.shape
    pieces, kinds, _, part, hidden = weights.shape
    row = lambda n: pl.BlockSpec((1, sources, slots, n), lambda e: (e, 0, 0, 0))
    weight = pl.BlockSpec((pieces, kinds, 1, part, hidden), lambda e: (0, 0, e, 0, 0))
    return pl.pallas_call(
        expert_kernel,
        grid=(experts,),
        in_specs=[row(width), row(width), row(128), weight],
        out_specs=[row(width), row(width), row(128), weight],
        out_shape=[
            jax.ShapeDtypeStruct(rows.shape, bf16),
            jax.ShapeDtypeStruct(rows.shape, bf16),
            jax.ShapeDtypeStruct(gates.shape, f32),
            jax.ShapeDtypeStruct(weights.shape, bf16),
        ],
        compiler_params=params(1),
        cost_estimate=pl.CostEstimate(
            flops=18 * experts * sources * slots * width * hidden,
            bytes_accessed=8 * experts * sources * slots * width + 4 * weights.size,
            transcendentals=experts * sources * slots * hidden,
        ),
        name="experts",
    )(rows, grads, gates, weights)


def combine_kernel(slot_ref, rows_ref, out_ref, picks_ref):
    experts, length = slot_ref.shape[1:]
    for expert in range(experts):
        match = lax.broadcasted_iota(jnp.int32, (MOST, length), 0) == slot_ref[0, expert : expert + 1, :]
        picks_ref[expert * MOST : (expert + 1) * MOST, :] = match.astype(f32).astype(bf16)
    rows = rows_ref[:, 0].reshape(experts * MOST, rows_ref.shape[3])
    out_ref[0] = dot(picks_ref[...], rows, 0, 0).astype(bf16)


def combine_gates_kernel(slot_ref, rows_ref, gate_ref, out_ref, gate_out_ref, picks_ref):
    combine_kernel(slot_ref, rows_ref, out_ref, picks_ref)
    experts, length = slot_ref.shape[1:]
    for expert in range(experts):
        match = lax.broadcasted_iota(jnp.int32, (MOST, length), 0) == slot_ref[0, expert : expert + 1, :]
        column = gate_ref[expert, 0][:, :1]
        gate_out_ref[0, expert : expert + 1, :] = jnp.sum(
            jnp.where(match, column, 0.0), axis=0, keepdims=True
        )


def run_combine(slots, rows, gate_grads=None):
    sources, experts, length = slots.shape
    width = rows.shape[3]
    table = pl.BlockSpec((1, experts, length), lambda s: (s, 0, 0))
    row = lambda n: pl.BlockSpec((experts, 1, MOST, n), lambda s: (0, s, 0, 0))
    out_spec = pl.BlockSpec((1, length, width), lambda s: (s, 0, 0))
    out_shape = jax.ShapeDtypeStruct((sources, length, width), bf16)
    common = dict(
        grid=(sources,),
        scratch_shapes=[pltpu.VMEM((experts * MOST, length), bf16)],
        compiler_params=params(1),
        cost_estimate=pl.CostEstimate(
            flops=2 * sources * experts * MOST * length * width,
            bytes_accessed=2 * rows.size + 2 * sources * length * width,
            transcendentals=0,
        ),
    )
    if gate_grads is None:
        return pl.pallas_call(
            combine_kernel,
            in_specs=[table, row(width)],
            out_specs=out_spec,
            out_shape=out_shape,
            name="combine",
            **common,
        )(slots, rows)
    return pl.pallas_call(
        combine_gates_kernel,
        in_specs=[table, row(width), row(128)],
        out_specs=[out_spec, table],
        out_shape=[out_shape, jax.ShapeDtypeStruct(slots.shape, f32)],
        name="combine_gates",
        **common,
    )(slots, rows, gate_grads)


def inverse_norm(values):
    return lax.rsqrt(jnp.mean(values * values, axis=-1, keepdims=True) + norm_epsilon)


def norm_back(incoming, values, inverse, gain_row):
    scaled = incoming * gain_row
    mean = jnp.mean(scaled * values, axis=-1, keepdims=True)
    grad = inverse * scaled - values * (inverse * inverse * inverse * mean)
    return grad, jnp.sum(incoming * values * inverse, axis=0)


def join_parts(parts, joined, cuts):
    if joined == 1:
        return parts
    count, width, _ = parts.shape
    pieces = jnp.split(parts, cuts, axis=2)
    return jnp.concatenate(
        [
            piece.reshape(count // joined, joined, width, -1)
            .transpose(0, 2, 1, 3)
            .reshape(count // joined, width, -1)
            for piece in pieces
        ],
        axis=2,
    )


def split_parts(parts, joined, cuts):
    if joined == 1:
        return parts
    count, width, _ = parts.shape
    pieces = jnp.split(parts, [cut * joined for cut in cuts], axis=2)
    return jnp.concatenate(
        [
            piece.reshape(count, width, joined, -1)
            .transpose(0, 2, 1, 3)
            .reshape(count * joined, width, -1)
            for piece in pieces
        ],
        axis=2,
    )


def shards(
    tokens,
    query_weight,
    key_projection,
    value_projection,
    output_weight,
    router_weight,
    attention_gain,
    mixture_gain,
    gate_weight,
    up_weight,
    down_weight,
    choices,
    cotangent,
):
    col_count, row_count, sources = (lax.axis_size(name) for name in ("col", "row", "expert"))
    length, width = tokens.shape
    query_width, key_width, output_width = (
        query_weight.shape[1],
        key_projection.shape[1],
        output_weight.shape[1],
    )
    router_width = router_weight.shape[1]
    local_experts = gate_weight.shape[1]
    inner = query_width + 2 * key_width

    gains = lax.all_gather(jnp.stack([attention_gain, mixture_gain]), ("row", "col"), axis=1, tiled=True)
    packed = jnp.concatenate(
        [query_weight, key_projection, value_projection, output_weight, router_weight], axis=1
    )
    packed = lax.all_gather(packed, ("col", "row"), axis=0, tiled=True)
    packed = packed.reshape(col_count, width, packed.shape[1])
    joined = max(1, 128 // key_width)
    cuts = (query_width, query_width + key_width)
    inner_weight = join_parts(packed[:, :, :inner], joined, cuts)
    outer_weight = packed[:, :, inner : inner + output_width]
    router_parts = packed[:, :, inner + output_width :]
    router_full = router_parts.transpose(1, 0, 2).reshape(width, EXPERTS)

    choices_all = lax.all_gather(choices, "expert", axis=0)
    cotangent_all = lax.all_gather(cotangent, "expert", axis=0)
    weights = jnp.stack([gate_weight, up_weight, down_weight]).transpose(0, 2, 1, 3)
    weights_all = lax.all_gather(weights, ("row", "col"), axis=0)

    expert_ids = jnp.arange(EXPERTS, dtype=jnp.int32)
    chosen = jnp.any(
        choices_all.transpose(0, 2, 1)[:, :, None, :] == expert_ids[None, None, :, None], axis=1
    )
    earlier = (jnp.arange(length)[:, None] < jnp.arange(length)[None, :]).astype(bf16)
    ranks = jnp.einsum("set,tu->seu", chosen.astype(bf16), earlier, preferred_element_type=f32)
    slots_all = jnp.where(chosen, ranks.astype(jnp.int32), -1)
    source = lax.axis_index("expert")
    slots = lax.dynamic_slice_in_dim(slots_all, source * local_experts, local_experts, axis=1)

    cosine, sine = rotary_tables(length)
    attention_full, mixture_full = gains[0].astype(f32), gains[1].astype(f32)
    inputs = tokens.astype(f32)
    first_inverse = inverse_norm(inputs)
    normed = (attention_full * inputs * first_inverse).astype(bf16)
    qkv = jnp.einsum("td,cdf->ctf", normed, inner_weight, preferred_element_type=f32)
    query_rot, key_rot, value_low, mixed, logs = run_forward(
        qkv, cosine, sine, query_width * joined, key_width * joined
    )
    branch = jnp.concatenate(
        [jnp.dot(mixed, outer_weight[c], preferred_element_type=f32) for c in range(col_count)], axis=1
    )
    middle = inputs + branch_factor * branch
    second_inverse = inverse_norm(middle)
    second = (mixture_full * middle * second_inverse).astype(bf16)

    second_all = lax.all_gather(second, "expert", axis=0)
    logits = jnp.einsum("de,std->set", router_full, second_all, preferred_element_type=f32)
    top = jnp.max(jnp.where(chosen, logits, masked_score), axis=1, keepdims=True)
    exped = jnp.where(chosen, jnp.exp(jnp.where(chosen, logits - top, 0.0)), 0.0)
    gates_all = exped / jnp.sum(exped, axis=1, keepdims=True)
    gates = lax.dynamic_slice_in_dim(gates_all, source * local_experts, local_experts, axis=1)
    own_gates = lax.dynamic_index_in_dim(gates_all, source, axis=0, keepdims=False)

    rows, grads, slot_gates = run_dispatch(slots, gates, second_all, cotangent_all)
    outs, backs, slot_gate_grads, weight_grads = run_experts(rows, grads, slot_gates, weights_all)
    back_sums, gate_grads = run_combine(slots, backs, slot_gate_grads)
    gate_grads = lax.all_to_all(gate_grads, "expert", split_axis=0, concat_axis=0).reshape(EXPERTS, length)
    second_grad = lax.psum_scatter(back_sums, "expert", scatter_dimension=0).astype(f32)
    out_sums = run_combine(slots, outs)
    combined = lax.psum_scatter(out_sums, "expert", scatter_dimension=0).astype(f32)
    layer_output = (middle + combined).astype(bf16)
    expert_sums = lax.psum_scatter(weight_grads, ("row", "col"), scatter_dimension=0)
    expert_sums = expert_sums.transpose(0, 2, 1, 3).astype(f32)

    mean_grad = jnp.sum(own_gates * gate_grads, axis=0, keepdims=True)
    logit_grad = (own_gates * (gate_grads - mean_grad)).astype(bf16)
    router_part = jnp.einsum("td,et->de", second, logit_grad, preferred_element_type=f32)
    second_grad = second_grad + jnp.einsum(
        "et,de->td", logit_grad, router_full, preferred_element_type=f32
    )
    middle_norm_grad, mixture_part = norm_back(second_grad, middle, second_inverse, mixture_full)
    middle_grad = cotangent.astype(f32) + middle_norm_grad
    branch_grad = (branch_factor * middle_grad).astype(bf16)
    branch_parts = [
        branch_grad[:, c * output_width : (c + 1) * output_width] for c in range(col_count)
    ]
    mixed_grad = sum(
        jnp.einsum("td,fd->tf", branch_parts[c], outer_weight[c], preferred_element_type=f32)
        for c in range(col_count)
    ).astype(bf16)
    output_parts = jnp.stack(
        [
            jnp.concatenate(
                [
                    jnp.einsum("tf,td->fd", mixed, branch_parts[c], preferred_element_type=f32),
                    router_part[:, c * router_width : (c + 1) * router_width],
                ],
                axis=1,
            ).astype(bf16)
            for c in range(col_count)
        ]
    )
    outer_sums = lax.psum_scatter(
        output_parts.reshape(col_count * width, -1), ("col", "row"), scatter_dimension=0, tiled=True
    )
    outer_sums = lax.psum(outer_sums, "expert").astype(f32)

    inner_grad = run_backward(query_rot, key_rot, value_low, mixed_grad, logs, cosine, sine)
    inner_parts = jnp.einsum(
        "td,ctf->cdf", normed, inner_grad, preferred_element_type=f32
    ).astype(bf16)
    inner_parts = split_parts(inner_parts, joined, cuts)
    inner_sums = lax.psum_scatter(
        inner_parts.reshape(col_count * width, -1), ("col", "row"), scatter_dimension=0, tiled=True
    )
    inner_sums = lax.psum(inner_sums, "expert").astype(f32)
    normed_grad = sum(
        jnp.einsum("tf,df->td", inner_grad[c], inner_weight[c], preferred_element_type=f32)
        for c in range(inner_grad.shape[0])
    )
    input_norm_grad, attention_part = norm_back(normed_grad, inputs, first_inverse, attention_full)
    input_gradient = middle_grad + input_norm_grad

    gain_sums = lax.psum(jnp.stack([attention_part, mixture_part]), ("row", "col", "expert"))
    gain_width = attention_gain.shape[0]
    place = lax.axis_index("row") * col_count + lax.axis_index("col")
    gain_sums = lax.dynamic_slice_in_dim(gain_sums, place * gain_width, gain_width, axis=1)
    return (
        layer_output,
        input_gradient,
        inner_sums[:, :query_width],
        inner_sums[:, query_width : query_width + key_width],
        inner_sums[:, query_width + key_width :],
        outer_sums[:, :output_width],
        outer_sums[:, output_width:],
        gain_sums[0],
        gain_sums[1],
        expert_sums[0],
        expert_sums[1],
        expert_sums[2],
    )


def solution(mesh):
    placed = (
        P(("row", "col", "expert"), None),
        P("row", "col"),
        P("row", "col"),
        P("row", "col"),
        P("row", "col"),
        P("row", "col"),
        P(("row", "col")),
        P(("row", "col")),
        P(("row", "col"), "expert", None),
        P(("row", "col"), "expert", None),
        P(("row", "col"), "expert", None),
        P(("row", "col", "expert"), None),
        P(("row", "col", "expert"), None),
    )
    return jax.shard_map(
        shards,
        mesh=mesh,
        in_specs=placed,
        out_specs=(
            P(("row", "col", "expert"), None),
            P(("row", "col", "expert"), None),
            P("row", "col"),
            P("row", "col"),
            P("row", "col"),
            P("row", "col"),
            P("row", "col"),
            P(("row", "col")),
            P(("row", "col")),
            P(("row", "col"), "expert", None),
            P(("row", "col"), "expert", None),
            P(("row", "col"), "expert", None),
        ),
        check_vma=False,
    )
```

time: 1760 us -> 951 us (0.54)
  waiting for transfers between devices: 1000 us -> 611 us
  local copies, waits for them, and re-layouts: 269 us -> 30.2 us
  matrix products: 242 us -> 39.4 us
  Pallas kernels: 0 us -> 149 us
  other arithmetic: 125 us -> 16.1 us
    all_to_all x4 -> x1, waiting for transfers between devices: 732 us -> 9 us  [shards(): lax.all_to_all(gate_grads, 'expert', split_axis=0, concat_axis=0)]
    all_gather x7 -> x4, waiting for transfers between devices: 0.03 us -> 260 us  [the longest x1 98.9 us: shards(): weights_all = lax.all_gather(weights, ('row', 'col'), axis=0)]
    dot_general x80 -> x14, matrix products: 242 us -> 39.4 us  [the longest x2 7.92 us: shards(): jnp.einsum('tf,df->td', inner_grad[c], inner_weight[c], preferred_element...]
    reduce_scatter x10 -> x5, waiting for transfers between devices: 147 us -> 297 us  [the longest x1 155 us: shards(): lax.psum_scatter(weight_grads, ('row', 'col'), scatter_dimension=0)]
    pallas_call x0 -> x6, Pallas kernels: none -> 149 us  [the longest x1 58.4 us: run_experts(): pl.pallas_call(expert_kernel, grid=(experts,), in_specs=[row(width), row(...]
    unnamed x20 -> x10, waiting for transfers between devices: 122 us -> 1.34 us
    gather x4 -> x0, local copies, waits for them, and re-layouts: 92.2 us -> none  [the longest x1 26.1 us: shards(): returned_grads[slot_index].reshape(sequence_length, TOP, -1)]
    all_to_all x4 -> x0, local copies, waits for them, and re-layouts: 43.7 us -> none  [the longest x1 12.8 us: shards(): lax.all_to_all(expert_out, 'expert', split_axis=1, concat_axis=0, tiled=T...]
  transfers between devices with their start and end apart: 23 -> 11, of which waited for: 13 -> 10; matrix products, arithmetic and copies ran while one was open for 24% -> 5% of each run, Pallas kernels for 0% -> 6%
where the time goes in v1:
time: 951 us; the launch traced here: 941 us
  waiting for transfers between devices  611 us (64%)
  Pallas kernels  149 us (16%)
  blocking collectives  65.7 us (7%)
  matrix products  39.4 us (4%)
  local copies, waits for them, and re-layouts  30.2 us (3%)
  other arithmetic  16.1 us (2%)
  starting transfers between devices  15.2 us (2%)
  between operations  14.8 us (2%)
    reduce_scatter x1, waiting for transfers between devices, shards(): lax.psum_scatter(weight_grads, ('row', 'col'), scatter_dimension=0)  155 us
    all_gather x1, waiting for transfers between devices, shards(): weights_all = lax.all_gather(weights, ('row', 'col'), axis=0)  98.9 us
    all_gather x1, waiting for transfers between devices, shards(): cotangent_all = lax.all_gather(cotangent, 'expert', axis=0)  76 us
    reduce_scatter x1, waiting for transfers between devices, shards(): lax.psum_scatter(back_sums, 'expert', scatter_dimension=0).astype(f32)  62 us
    pallas_call x1, Pallas kernels, run_experts(): pl.pallas_call(expert_kernel, grid=(experts,), in_specs=[row(width), row(...  58.4 us
    reduce_scatter x1, waiting for transfers between devices, shards(): lax.psum_scatter(inner_parts.reshape(col_count * width, -1), ('col', 'row...  51.2 us
    all_gather x1, waiting for transfers between devices, shards(): second_all = lax.all_gather(second, 'expert', axis=0)  47.4 us
    psum x1, waiting for transfers between devices, shards(): inner_sums = lax.psum(inner_sums, 'expert').astype(f32)  43.3 us
  transfers between devices with their start and end apart: 11, of which 10 were waited for; matrix products, arithmetic and copies ran while one was open for 5% of the time, Pallas kernels for 6%

profile of v1, /device:TPU:0, one launch (start us, length us, event | category | flops | bytes accessed | tf_op | source)
XLA Modules:
  0.0 941.4 jit_solution(12170480691771479664)
XLA Ops:
  13.0 10.2 %all_gather.31 = bf16[2,1024]{1,0:T(2,128)(2,1)S(1)} all-gather(bf16[2,128]{1,0:T(2,128)(2,1)S(1)} %pad_maximum_fusion.3), channel_id=1, replica_groups=mesh['row'=4,'col'=2,'expert'=4] {'row','col'}, dimensions={1}, use_global_device_ids=true | all-gather | bytes 4608 | tf_op jit(solution)/shard_map/all_gather | solution.py:423
  25.8 37.7 %all-gather.9.cloned.1.call-done = bf16[2048,1552]{1,0:T(8,128)(2,1)} async-done(((bf16[256,1552]{1,0:T(8,128)(2,1)}), bf16[2048,1552]{1,0:T(8,128)(2,1)}) %all-gather.9.cloned.1.call-update) | async-done | bytes 6357008 | tf_op jit(solution)/shard_map/all_gather | solution.py:427
  63.5 6.5 fusion.3.qkv_ref
  70.0 21.0 %attention_forward.1 = (bf16[2,512,512]{2,1,0:T(8,128)(2,1)}, bf16[2,512,256]{2,1,0:T(8,128)(2,1)}, bf16[2,512,256]{2,1,0:T(8,128)(2,1)}, bf16[512,1024]{1,0:T(8,128)(2,1)}, f32[2,512,128]{2,1,0:T(8,128)}) custom-call(f32[2,512,1024]{2,1,0:T(8,128)} %fusion.3.qkv_ref, f32[512,128]{1,0:T(8,128)} %get-tuple-element.128.cos_ref, ...), custom_call_target="tpu_custom_call" | custom-call | flops 1073741824 | bytes 8388608 | tf_op jit(solution)/shard_map/attention_forward/pallas_call | solution.py:140
  97.8 10.3 %all-gather.15.cloned.1.call-start = ((), (), s32[]{:S(2)}) async-start(), calls=%async_computation.14 | async-start | bytes 28311552 | tf_op jit(solution)/shard_map/all_gather | solution.py:439
  113.5 13.6 %all-gather = s32[2048,8]{0,1:T(8,128)S(1)} all-gather(s32[512,8]{0,1:T(8,128)S(1)} %copy-done.16), channel_id=2, replica_groups=mesh['row'=4,'col'=2,'expert'=4] {'expert'}, dimensions={0}, use_global_device_ids=true | all-gather | bytes 81920 | tf_op jit(solution)/shard_map/all_gather | solution.py:436
  131.5 47.4 %all-gather.11.cloned.1.call-done = bf16[2048,1024]{1,0:T(8,128)(2,1)} async-done(((bf16[512,1024]{1,0:T(8,128)(2,1)}), bf16[2048,1024]{1,0:T(8,128)(2,1)}) %all-gather.11.cloned.1.call-update) | async-done | bytes 4194320 | tf_op jit(solution)/shard_map/all_gather | solution.py:467
  183.9 76.0 %all-gather.13.cloned.1.call-done = bf16[2048,1024]{1,0:T(8,128)(2,1)} async-done(((bf16[512,1024]{1,0:T(8,128)(2,1)}), bf16[2048,1024]{1,0:T(8,128)(2,1)}) %all-gather.13.cloned.1.call-update) | async-done | bytes 4194320 | tf_op jit(solution)/shard_map/all_gather | solution.py:437
  259.9 26.7 %dispatch.1 = (bf16[8,4,144,1024]{3,2,1,0:T(8,128)(2,1)}, bf16[8,4,144,1024]{3,2,1,0:T(8,128)(2,1)}, f32[8,4,144,128]{3,2,1,0:T(8,128)}) custom-call(s32[4,8,512]{2,1,0:T(8,128)} %fusion.43.slot_ref, f32[4,8,512]{2,1,0:T(8,128)} %constant_dynamic-slice_fusion.1.gate_ref, bf16[4,512,1024]{2,1,0:T(8,128)(2,1)} %bitcast.140, bf16[4,512,1024]{2,1,0:T(8,128)(2,1)} %bitcast.167), custom_call_target="tpu_custom_call" | custom-call | flops 9663676416 | bytes 18874368 | tf_op jit(solution)/shard_map/dispatch/pallas_call | solution.py:221
  286.6 98.9 %all-gather.15.cloned.1.call-done = bf16[24,8,128,512]{3,2,1,0:T(8,128)(2,1)} async-done(((bf16[3,8,128,512]{3,2,1,0:T(8,128)(2,1)}), bf16[24,8,128,512]{3,2,1,0:T(8,128)(2,1)}) %all-gather.15.cloned.1.call-update) | async-done | bytes 25165840 | tf_op jit(solution)/shard_map/all_gather | solution.py:439
  385.5 58.4 %experts.1 = (bf16[8,4,144,1024]{3,2,1,0:T(8,128)(2,1)}, bf16[8,4,144,1024]{3,2,1,0:T(8,128)(2,1)}, f32[8,4,144,128]{3,2,1,0:T(8,128)}, bf16[8,3,8,128,512]{4,3,2,1,0:T(8,128)(2,1)}) custom-call(bf16[8,4,144,1024]{3,2,1,0:T(8,128)(2,1)} %get-tuple-element.27.rows_ref, bf16[8,4,144,1024]{3,2,1,0:T(8,128)(2,1)} %get-tuple-element.28.grads_ref, ...), custom_call_target="tpu_custom_call" | custom-call | flops 43486543872 | bytes 88080384 | tf_op jit(solution)/shard_map/experts/pallas_call | solution.py:277
  443.9 10.0 %combine_gates.1 = (bf16[4,512,1024]{2,1,0:T(8,128)(2,1)}, f32[4,8,512]{2,1,0:T(8,128)}) custom-call(s32[4,8,512]{2,1,0:T(8,128)} %fusion.43.slot_ref, bf16[8,4,144,1024]{3,2,1,0:T(8,128)(2,1)} %get-tuple-element.31.rows_ref, f32[8,4,144,128]{3,2,1,0:T(8,128)} %get-tuple-element.32.gate_ref), custom_call_target="tpu_custom_call" | custom-call | flops 4831838208 | bytes 13631488 | tf_op jit(solution)/shard_map/combine_gates/pallas_call | solution.py:344
  454.0 4.6 all-to-all-start
  458.6 9.0 all-to-all-done
  469.8 62.0 %reduce-scatter.8.cloned.1.call-done = bf16[1,512,1024]{2,1,0:T(8,128)(2,1)} async-done(((bf16[4,512,1024]{2,1,0:T(8,128)(2,1)}), bf16[1,512,1024]{2,1,0:T(8,128)(2,1)}) %reduce-scatter.8.cloned.1.call-update) | async-done | bytes 1048592 | tf_op jit(solution)/shard_map/reduce_scatter | solution.py:479
  545.1 23.3 %attention_backward.1 = bf16[2,512,1024]{2,1,0:T(8,128)(2,1)} custom-call(bf16[2,512,512]{2,1,0:T(8,128)(2,1)} %get-tuple-element.35.query_ref, bf16[2,512,256]{2,1,0:T(8,128)(2,1)} %get-tuple-element.36.key_ref, bf16[2,512,256]{2,1,0:T(8,128)(2,1)} %get-tuple-element.37.value_ref, bf16[512,1024]{1,0:T(8,128)(2,1)} %add_convert_fusion.grad_ref, ...), custom_call_target="tpu_custom_call" | custom-call | flops 2684354560 | bytes 6291456 | tf_op jit(solution)/shard_map/attention_backward/pallas_call | solution.py:174
  568.4 6.0 convolution_convert_fusion
  574.5 9.8 %combine.1 = bf16[4,512,1024]{2,1,0:T(8,128)(2,1)} custom-call(s32[4,8,512]{2,1,0:T(8,128)} %fusion.43.slot_ref, bf16[8,4,144,1024]{3,2,1,0:T(8,128)(2,1)} %get-tuple-element.30.rows_ref), custom_call_target="tpu_custom_call" | custom-call | flops 4831838208 | bytes 13631488 | tf_op jit(solution)/shard_map/combine/pallas_call | solution.py:336
  584.4 51.2 %reduce-scatter.10.cloned.1.call-done = bf16[256,1024]{1,0:T(8,128)(2,1)} async-done(((bf16[2048,1024]{1,0:T(8,128)(2,1)}), bf16[256,1024]{1,0:T(8,128)(2,1)}) %reduce-scatter.10.cloned.1.call-update) | async-done | bytes 524304 | tf_op jit(solution)/shard_map/reduce_scatter | solution.py:524
  639.6 4.6 fusion.13
  644.2 41.9 %psum.23 = f32[2,1024]{1,0:T(2,128)S(1)} all-reduce(f32[2,1024]{1,0:T(2,128)S(1)} %pad_maximum_fusion.2), channel_id=1, replica_groups=mesh['row'=4,'col'=2,'expert'=4] {'row','col','expert'}, use_global_device_ids=true, to_apply=%region_16.17 | all-reduce | flops 2048 | bytes 16384 | tf_op jit(solution)/shard_map/psum | solution.py:535
  686.6 29.2 %reduce-scatter.6.cloned.1.call-done = bf16[1,512,1024]{2,1,0:T(8,128)(2,1)} async-done(((bf16[4,512,1024]{2,1,0:T(8,128)(2,1)}), bf16[1,512,1024]{2,1,0:T(8,128)(2,1)}) %reduce-scatter.6.cloned.1.call-update) | async-done | bytes 1048592 | tf_op jit(solution)/shard_map/reduce_scatter | solution.py:481
  720.3 43.3 %all-reduce.3.cloned.1.call-done = (bf16[256,1024]{1,0:T(8,128)(2,1)}, bf16[256,528]{0,1:T(8,128)(2,1)}) async-done(((bf16[256,1024]{1,0:T(8,128)(2,1)}, bf16[256,528]{0,1:T(8,128)(2,1)}), (bf16[256,1024]{1,0:T(8,128)(2,1)}, bf16[256,528]{0,1:T(8,128)(2,1)})) %all-reduce.3.cloned.1.call-update) | async-done | bytes 794640 | tf_op jit(solution)/shard_map/psum | solution.py:527
  768.6 154.6 %reduce-scatter.14.cloned.1.call-done = bf16[1,3,8,128,512]{4,3,2,1,0:T(8,128)(2,1)} async-done(((bf16[8,3,8,128,512]{4,3,2,1,0:T(8,128)(2,1)}), bf16[1,3,8,128,512]{4,3,2,1,0:T(8,128)(2,1)}) %reduce-scatter.14.cloned.1.call-update) | async-done | bytes 3145744 | tf_op jit(solution)/shard_map/reduce_scatter | solution.py:483
  (127 shorter events, 70.2 us)
Async XLA Ops:
  7.2 5.8 copy-start.19
  7.2 5.8 copy-start.20
  7.2 56.3 %all-gather.9.cloned.1.call-start = ((), (), s32[]{:S(2)}) async-start(), calls=%async_computation.6 | async-start | bytes 7667712 | tf_op jit(solution)/shard_map/all_gather | solution.py:427
  9.0 16.4 %copy-start.1 = (bf16[512,1024]{1,0:T(8,128)(2,1)S(1)}, bf16[512,1024]{1,0:T(8,128)(2,1)}, u32[]{:S(2)}) copy-start(bf16[512,1024]{1,0:T(8,128)(2,1)} %param.13) | copy-start | bytes 3145732
  12.9 166.0 %all-gather.11.cloned.1.call-start = ((), (), s32[]{:S(2)}) async-start(), calls=%async_computation.12 | async-start | bytes 5242880 | tf_op jit(solution)/shard_map/all_gather | solution.py:467
  25.8 44.3 %copy-start.17 = (f32[512]{0:T(512)}, f32[512]{0:T(512)S(1)}, u32[]{:S(2)}) copy-start(f32[512]{0:T(512)S(1)} %add_rsqrt_fusion.1) | copy-start | bytes 6148
  25.8 44.2 %copy-start.13 = (f32[1,1024]{1,0:T(1,128)}, f32[1,1024]{1,0:T(1,128)S(1)}, u32[]{:S(2)}) copy-start(f32[1,1024]{1,0:T(1,128)S(1)} %get-tuple-element.118) | copy-start | bytes 12292
  91.0 2.3 copy-start.21
  97.0 162.9 %all-gather.13.cloned.1.call-start = ((), (), s32[]{:S(2)}) async-start(), calls=%async_computation.13 | async-start | bytes 5242880 | tf_op jit(solution)/shard_map/all_gather | solution.py:437
  97.8 287.8 %all-gather.15.cloned.1.call-start = ((), (), s32[]{:S(2)}) async-start(), calls=%async_computation.14 | async-start | bytes 28311552 | tf_op jit(solution)/shard_map/all_gather | solution.py:439
  112.8 419.0 %reduce-scatter.8.cloned.1.call-start = ((), (), s32[]{:S(2)}) async-start(), calls=%async_computation.8 | async-start | bytes 5242880 | tf_op jit(solution)/shard_map/reduce_scatter | solution.py:479
  454.0 13.6 %all-to-all-start = ((f32[4,8,512]{2,1,0:T(8,128)}), f32[4,8,512]{2,1,0:T(8,128)S(1)}, u32[]{:S(2)}, u32[]{:S(2)}) async-start(f32[4,8,512]{2,1,0:T(8,128)} %get-tuple-element.34), calls=%async_computation.2 | async-start | bytes 131072 | tf_op jit(solution)/shard_map/all_to_all | solution.py:478
  458.6 125.8 %reduce-scatter.12.cloned.1.call-start = ((), (), s32[]{:S(2)}) async-start(), calls=%async_computation.10 | async-start | bytes 2433024 | tf_op jit(solution)/shard_map/reduce_scatter | solution.py:514
  531.8 2.8 copy-start.12
  531.8 2.8 copy-start.2
  539.9 95.7 %reduce-scatter.10.cloned.1.call-start = ((), (), s32[]{:S(2)}) async-start(), calls=%async_computation.9 | async-start | bytes 4718592 | tf_op jit(solution)/shard_map/reduce_scatter | solution.py:524
  545.1 23.3 %copy-start.14 = (f32[1,1024]{1,0:T(1,128)S(1)}, f32[1,1024]{1,0:T(1,128)}, u32[]{:S(2)}) copy-start(f32[1,1024]{1,0:T(1,128)} %copy-done.13) | copy-start | bytes 12292
  545.1 23.3 %copy-start.18 = (f32[512]{0:T(512)S(1)}, f32[512]{0:T(512)}, u32[]{:S(2)}) copy-start(f32[512]{0:T(512)} %copy-done.17) | copy-start | bytes 6148
  574.4 141.4 %reduce-scatter.6.cloned.1.call-start = ((), (), s32[]{:S(2)}) async-start(), calls=%async_computation.7 | async-start | bytes 5242880 | tf_op jit(solution)/shard_map/reduce_scatter | solution.py:481
  584.3 179.3 %all-reduce.3.cloned.1.call-start = ((), (), s32[]{:S(2)}) async-start(), calls=%async_computation.15 | async-start | bytes 1589248 | tf_op jit(solution)/shard_map/psum | solution.py:527
  635.6 287.6 %reduce-scatter.14.cloned.1.call-start = ((), (), s32[]{:S(2)}) async-start(), calls=%async_computation.11 | async-start | bytes 28311552 | tf_op jit(solution)/shard_map/reduce_scatter | solution.py:483
  636.2 3.4 copy-start.23
  639.6 4.6 copy-start.15
  763.6 3.4 copy-start.5
  (11 other events, 15.1 us)
Sparse Core Ops, SparseCore 0:
  13.0 50.4 all-gather.8
  97.1 81.7 all-gather.10
  180.5 79.3 all-gather.12
  261.6 123.8 all-gather.14
  454.1 77.6 reduce-scatter.7
  540.0 40.8 reduce-scatter.11
  584.3 51.3 reduce-scatter.9
  638.0 77.7 reduce-scatter.5
  718.3 45.2 all-reduce.2
  767.0 156.1 reduce-scatter.13

commit v2 on v1

--- a/solution.py
+++ b/solution.py
@@ -394,6 +394,29 @@
     )
 
 
+def shifted(values, shift, count):
+    return lax.ppermute(values, "expert", [(i, (i + shift) % count) for i in range(count)])
+
+
+def gather_steps(values, count):
+    me = lax.axis_index("expert")
+    whole = jnp.zeros((count,) + values.shape, values.dtype)
+    for shift in range(count):
+        piece = shifted(values, shift, count) if shift else values
+        whole = lax.dynamic_update_index_in_dim(whole, piece, (me - shift + count) % count, 0)
+    return whole
+
+
+def sum_steps(values, count):
+    me = lax.axis_index("expert")
+    total = None
+    for shift in range(count):
+        piece = lax.dynamic_index_in_dim(values, (me + shift) % count, axis=0, keepdims=False)
+        piece = (shifted(piece, shift, count) if shift else piece).astype(f32)
+        total = piece if total is None else total + piece
+    return total
+
+
 def shards(
     tokens,
     query_weight,
@@ -434,7 +457,7 @@
     router_full = router_parts.transpose(1, 0, 2).reshape(width, EXPERTS)
 
     choices_all = lax.all_gather(choices, "expert", axis=0)
-    cotangent_all = lax.all_gather(cotangent, "expert", axis=0)
+    cotangent_all = gather_steps(cotangent, sources)
     weights = jnp.stack([gate_weight, up_weight, down_weight]).transpose(0, 2, 1, 3)
     weights_all = lax.all_gather(weights, ("row", "col"), axis=0)
 
@@ -464,6 +487,7 @@
     second_inverse = inverse_norm(middle)
     second = (mixture_full * middle * second_inverse).astype(bf16)
 
+    second, weights_all = lax.optimization_barrier((second, weights_all))
     second_all = lax.all_gather(second, "expert", axis=0)
     logits = jnp.einsum("de,std->set", router_full, second_all, preferred_element_type=f32)
     top = jnp.max(jnp.where(chosen, logits, masked_score), axis=1, keepdims=True)
@@ -476,12 +500,11 @@
     outs, backs, slot_gate_grads, weight_grads = run_experts(rows, grads, slot_gates, weights_all)
     back_sums, gate_grads = run_combine(slots, backs, slot_gate_grads)
     gate_grads = lax.all_to_all(gate_grads, "expert", split_axis=0, concat_axis=0).reshape(EXPERTS, length)
-    second_grad = lax.psum_scatter(back_sums, "expert", scatter_dimension=0).astype(f32)
+    second_grad = sum_steps(back_sums, sources)
     out_sums = run_combine(slots, outs)
-    combined = lax.psum_scatter(out_sums, "expert", scatter_dimension=0).astype(f32)
+    combined = sum_steps(out_sums, sources)
     layer_output = (middle + combined).astype(bf16)
     expert_sums = lax.psum_scatter(weight_grads, ("row", "col"), scatter_dimension=0)
-    expert_sums = expert_sums.transpose(0, 2, 1, 3).astype(f32)
 
     mean_grad = jnp.sum(own_gates * gate_grads, axis=0, keepdims=True)
     logit_grad = (own_gates * (gate_grads - mean_grad)).astype(bf16)
@@ -511,6 +534,7 @@
             for c in range(col_count)
         ]
     )
+    output_parts, expert_sums = lax.optimization_barrier((output_parts, expert_sums))
     outer_sums = lax.psum_scatter(
         output_parts.reshape(col_count * width, -1), ("col", "row"), scatter_dimension=0, tiled=True
     )
@@ -533,6 +557,7 @@
     input_gradient = middle_grad + input_norm_grad
 
     gain_sums = lax.psum(jnp.stack([attention_part, mixture_part]), ("row", "col", "expert"))
+    expert_sums = expert_sums.transpose(0, 2, 1, 3).astype(f32)
     gain_width = attention_gain.shape[0]
     place = lax.axis_index("row") * col_count + lax.axis_index("col")
     gain_sums = lax.dynamic_slice_in_dim(gain_sums, place * gain_width, gain_width, axis=1)

time: 951 us -> 826 us (0.87)
  waiting for transfers between devices: 611 us -> 247 us
  blocking collectives: 65.7 us -> 274 us
  local copies, waits for them, and re-layouts: 30.2 us -> 51.5 us
    reduce_scatter x1, waiting for transfers between devices: 155 us -> 2.18 us  [shards(): lax.psum_scatter(weight_grads, ('row', 'col'), scatter_dimension=0)]
    all_gather x1, blocking collectives: 13.6 us -> 162 us  [shards(): choices_all = lax.all_gather(choices, 'expert', axis=0)]
    reduce_scatter x2 -> x0, waiting for transfers between devices: 91.2 us -> none  [the longest x1 62 us: shards(): lax.psum_scatter(back_sums, 'expert', scatter_dimension=0).astype(f32)]
    all_gather x1 -> x0, waiting for transfers between devices: 76 us -> none  [shards(): cotangent_all = lax.all_gather(cotangent, 'expert', axis=0)]
    all_to_all x1, waiting for transfers between devices: 9 us -> 84.3 us  [shards(): lax.all_to_all(gate_grads, 'expert', split_axis=0, concat_axis=0)]
    psum x1, blocking collectives: 41.9 us -> 101 us  [shards(): lax.psum(jnp.stack([attention_part, mixture_part]), ('row', 'col', 'exper...]
    reduce_scatter x1, waiting for transfers between devices: 51.2 us -> 0.01 us  [shards(): lax.psum_scatter(inner_parts.reshape(col_count * width, -1), ('col', 'row...]
    all_gather x1, waiting for transfers between devices: 47.4 us -> 0.02 us  [shards(): second_all = lax.all_gather(second, 'expert', axis=0)]
  transfers between devices with their start and end apart: 11 -> 17, of which waited for: 10 -> 5; matrix products, arithmetic and copies ran while one was open for 5% -> 11% of each run, Pallas kernels for 6% -> 8%
where the time goes in v2:
time: 826 us; the launch traced here: 815 us
  blocking collectives  274 us (33%)
  waiting for transfers between devices  247 us (30%)
  Pallas kernels  149 us (18%)
  local copies, waits for them, and re-layouts  51.5 us (6%)
  matrix products  41.4 us (5%)
  starting transfers between devices  18.8 us (2%)
  other arithmetic  18.6 us (2%)
  between operations  15 us (2%)
    all_gather x1, blocking collectives, shards(): choices_all = lax.all_gather(choices, 'expert', axis=0)  162 us
    psum x1, blocking collectives, shards(): lax.psum(jnp.stack([attention_part, mixture_part]), ('row', 'col', 'exper...  101 us
    all_gather x1, waiting for transfers between devices, shards(): weights_all = lax.all_gather(weights, ('row', 'col'), axis=0)  93.7 us
    all_to_all x1, waiting for transfers between devices, shards(): lax.all_to_all(gate_grads, 'expert', split_axis=0, concat_axis=0)  84.3 us
    pallas_call x1, Pallas kernels, run_experts(): pl.pallas_call(expert_kernel, grid=(experts,), in_specs=[row(width), row(...  58.4 us
    psum x1, waiting for transfers between devices, shards(): inner_sums = lax.psum(inner_sums, 'expert').astype(f32)  34.5 us
    all_gather x1, waiting for transfers between devices, shards(): packed = lax.all_gather(packed, ('col', 'row'), axis=0, tiled=True)  32.5 us
    pallas_call x1, Pallas kernels, run_dispatch(): pl.pallas_call(dispatch_kernel, grid=(sources, experts), in_specs=[table,...  26 us
  transfers between devices with their start and end apart: 17, of which 5 were waited for; matrix products, arithmetic and copies ran while one was open for 11% of the time, Pallas kernels for 8%

profile of v2, /device:TPU:0, one launch (start us, length us, event | category | flops | bytes accessed | tf_op | source)
XLA Modules:
  0.0 815.2 jit_solution(4290184538118320248)
XLA Ops:
  18.2 10.2 %all_gather.25 = bf16[2,1024]{1,0:T(2,128)(2,1)S(1)} all-gather(bf16[2,128]{1,0:T(2,128)(2,1)S(1)} %pad_maximum_fusion.3), channel_id=1, replica_groups=mesh['row'=4,'col'=2,'expert'=4] {'row','col'}, dimensions={1}, use_global_device_ids=true | all-gather | bytes 4608 | tf_op jit(solution)/shard_map/all_gather | solution.py:446
  31.0 32.5 %all-gather.7.cloned.1.call-done = bf16[2048,1552]{1,0:T(8,128)(2,1)} async-done(((bf16[256,1552]{1,0:T(8,128)(2,1)}), bf16[2048,1552]{1,0:T(8,128)(2,1)}) %all-gather.7.cloned.1.call-update) | async-done | bytes 6357008 | tf_op jit(solution)/shard_map/all_gather | solution.py:450
  63.5 6.6 fusion.3.qkv_ref
  70.0 21.1 %attention_forward.1 = (bf16[2,512,512]{2,1,0:T(8,128)(2,1)}, bf16[2,512,256]{2,1,0:T(8,128)(2,1)}, bf16[2,512,256]{2,1,0:T(8,128)(2,1)}, bf16[512,1024]{1,0:T(8,128)(2,1)}, f32[2,512,128]{2,1,0:T(8,128)}) custom-call(f32[2,512,1024]{2,1,0:T(8,128)} %fusion.3.qkv_ref, f32[512,128]{1,0:T(8,128)} %get-tuple-element.142.cos_ref, ...), custom_call_target="tpu_custom_call" | custom-call | flops 1073741824 | bytes 8388608 | tf_op jit(solution)/shard_map/attention_forward/pallas_call | solution.py:140
  97.1 93.7 %all-gather.9.cloned.1.call-done = bf16[24,8,128,512]{3,2,1,0:T(8,128)(2,1)} async-done(((bf16[3,8,128,512]{3,2,1,0:T(8,128)(2,1)}), bf16[24,8,128,512]{3,2,1,0:T(8,128)(2,1)}) %all-gather.9.cloned.1.call-update) | async-done | bytes 25165840 | tf_op jit(solution)/shard_map/all_gather | solution.py:462
  196.5 162.3 %all-gather = s32[2048,8]{0,1:T(8,128)S(1)} all-gather(s32[512,8]{0,1:T(8,128)S(1)} %copy-done.14), channel_id=2, replica_groups=mesh['row'=4,'col'=2,'expert'=4] {'expert'}, dimensions={0}, use_global_device_ids=true | all-gather | bytes 81920 | tf_op jit(solution)/shard_map/all_gather | solution.py:459
  373.8 3.5 convolution_bitcast_fusion
  378.7 26.0 %dispatch.1 = (bf16[8,4,144,1024]{3,2,1,0:T(8,128)(2,1)}, bf16[8,4,144,1024]{3,2,1,0:T(8,128)(2,1)}, f32[8,4,144,128]{3,2,1,0:T(8,128)}) custom-call(s32[4,8,512]{2,1,0:T(8,128)} %fusion.49.slot_ref, f32[4,8,512]{2,1,0:T(8,128)} %constant_dynamic-slice_fusion.1.gate_ref, bf16[4,512,1024]{2,1,0:T(8,128)(2,1)} %bitcast.160, ...), custom_call_target="tpu_custom_call" | custom-call | flops 9663676416 | bytes 18874368 | tf_op jit(solution)/shard_map/dispatch/pallas_call | solution.py:221
  404.7 58.4 %experts.1 = (bf16[8,4,144,1024]{3,2,1,0:T(8,128)(2,1)}, bf16[8,4,144,1024]{3,2,1,0:T(8,128)(2,1)}, f32[8,4,144,128]{3,2,1,0:T(8,128)}, bf16[8,3,8,128,512]{4,3,2,1,0:T(8,128)(2,1)}) custom-call(bf16[8,4,144,1024]{3,2,1,0:T(8,128)(2,1)} %get-tuple-element.32.rows_ref, bf16[8,4,144,1024]{3,2,1,0:T(8,128)(2,1)} %get-tuple-element.33.grads_ref, ...), custom_call_target="tpu_custom_call" | custom-call | flops 43486543872 | bytes 88080384 | tf_op jit(solution)/shard_map/experts/pallas_call | solution.py:277
  463.1 10.9 %combine_gates.1 = (bf16[4,512,1024]{2,1,0:T(8,128)(2,1)}, f32[4,8,512]{2,1,0:T(8,128)}) custom-call(s32[4,8,512]{2,1,0:T(8,128)} %fusion.49.slot_ref, bf16[8,4,144,1024]{3,2,1,0:T(8,128)(2,1)} %get-tuple-element.37.rows_ref, f32[8,4,144,128]{3,2,1,0:T(8,128)} %get-tuple-element.38.gate_ref), custom_call_target="tpu_custom_call" | custom-call | flops 4831838208 | bytes 13631488 | tf_op jit(solution)/shard_map/combine_gates/pallas_call | solution.py:344
  474.0 4.6 dynamic-slice_bitcast_fusion.2
  478.7 3.7 collective-permute-start.8
  482.4 4.2 all-to-all-start
  486.6 84.3 %all-to-all-done = f32[4,8,512]{2,1,0:T(8,128)S(1)} async-done(((f32[4,8,512]{2,1,0:T(8,128)}), f32[4,8,512]{2,1,0:T(8,128)S(1)}, u32[]{:S(2)}, u32[]{:S(2)}) %all-to-all-start) | async-done | bytes 65568 | tf_op jit(solution)/shard_map/all_to_all | solution.py:502
  571.0 4.2 multiply_reduce_fusion
  581.9 22.9 %attention_backward.1 = bf16[2,512,1024]{2,1,0:T(8,128)(2,1)} custom-call(bf16[2,512,512]{2,1,0:T(8,128)(2,1)} %get-tuple-element.41.query_ref, bf16[2,512,256]{2,1,0:T(8,128)(2,1)} %get-tuple-element.42.key_ref, bf16[2,512,256]{2,1,0:T(8,128)(2,1)} %get-tuple-element.43.value_ref, bf16[512,1024]{1,0:T(8,128)(2,1)} %add_convert_fusion.grad_ref, ...), custom_call_target="tpu_custom_call" | custom-call | flops 2684354560 | bytes 6291456 | tf_op jit(solution)/shard_map/attention_backward/pallas_call | solution.py:174
  604.7 6.1 convolution_convert_fusion
  619.2 3.2 copy.120
  622.5 9.6 %combine.1 = bf16[4,512,1024]{2,1,0:T(8,128)(2,1)} custom-call(s32[4,8,512]{2,1,0:T(8,128)} %fusion.49.slot_ref, bf16[8,4,144,1024]{3,2,1,0:T(8,128)(2,1)} %get-tuple-element.36.rows_ref), custom_call_target="tpu_custom_call" | custom-call | flops 4831838208 | bytes 13631488 | tf_op jit(solution)/shard_map/combine/pallas_call | solution.py:336
  632.1 4.0 dynamic-slice_bitcast_fusion.5
  643.6 5.0 fusion.13
  648.6 101.3 %psum.23 = f32[2,1024]{1,0:T(2,128)S(1)} all-reduce(f32[2,1024]{1,0:T(2,128)S(1)} %pad_maximum_fusion.2), channel_id=1, replica_groups=mesh['row'=4,'col'=2,'expert'=4] {'row','col','expert'}, use_global_device_ids=true, to_apply=%region_15.16 | all-reduce | flops 2048 | bytes 16384 | tf_op jit(solution)/shard_map/psum | solution.py:559
  750.5 5.6 fusion.11
  767.4 34.5 %all-reduce.3.cloned.1.call-done = (bf16[256,1024]{1,0:T(8,128)(2,1)}, bf16[256,528]{0,1:T(8,128)(2,1)}) async-done(((bf16[256,1024]{1,0:T(8,128)(2,1)}, bf16[256,528]{0,1:T(8,128)(2,1)}), (bf16[256,1024]{1,0:T(8,128)(2,1)}, bf16[256,528]{0,1:T(8,128)(2,1)})) %all-reduce.3.cloned.1.call-update) | async-done | bytes 794640 | tf_op jit(solution)/shard_map/psum | solution.py:551
  (143 shorter events, 81.9 us)
Async XLA Ops:
  7.2 56.3 %all-gather.7.cloned.1.call-start = ((), (), s32[]{:S(2)}) async-start(), calls=%async_computation.4 | async-start | bytes 7667712 | tf_op jit(solution)/shard_map/all_gather | solution.py:450
  12.9 177.8 %all-gather.9.cloned.1.call-start = ((), (), s32[]{:S(2)}) async-start(), calls=%async_computation.8 | async-start | bytes 28311552 | tf_op jit(solution)/shard_map/all_gather | solution.py:462
  17.5 13.2 %copy-start.2 = (bf16[512,1024]{1,0:T(8,128)(2,1)S(1)}, bf16[512,1024]{1,0:T(8,128)(2,1)}, u32[]{:S(2)}) copy-start(bf16[512,1024]{1,0:T(8,128)(2,1)} %param.13) | copy-start | bytes 3145732
  17.5 356.3 %all-gather.11.cloned.1.call-start = ((), (), s32[]{:S(2)}) async-start(), calls=%async_computation.9 | async-start | bytes 5242880 | tf_op jit(solution)/shard_map/all_gather | solution.py:491
  30.9 39.1 %copy-start.17 = (f32[512]{0:T(512)}, f32[512]{0:T(512)S(1)}, u32[]{:S(2)}) copy-start(f32[512]{0:T(512)S(1)} %add_rsqrt_fusion.1) | copy-start | bytes 6148
  31.0 39.1 %copy-start.15 = (f32[1,1024]{1,0:T(1,128)}, f32[1,1024]{1,0:T(1,128)S(1)}, u32[]{:S(2)}) copy-start(f32[1,1024]{1,0:T(1,128)S(1)} %get-tuple-element.132) | copy-start | bytes 12292
  95.8 100.7 %copy-start.14 = (s32[512,8]{0,1:T(8,128)S(1)}, s32[512,8]{0,1:T(8,128)}, u32[]{:S(2)}) copy-start(s32[512,8]{0,1:T(8,128)} %param.24) | copy-start | bytes 49156
  190.7 428.5 %reduce-scatter.6.cloned.1.call-start = ((), (), s32[]{:S(2)}) async-start(), calls=%async_computation.6 | async-start | bytes 28311552 | tf_op jit(solution)/shard_map/reduce_scatter | solution.py:507
  190.8 173.0 %collective-permute-start = (bf16[512,1024]{1,0:T(8,128)(2,1)}, bf16[512,1024]{1,0:T(8,128)(2,1)}, u32[]{:S(2)}, u32[]{:S(2)}) collective-permute-start(bf16[512,1024]{1,0:T(8,128)(2,1)} %param.25), channel_id=1, source_target_pairs={{0,1},{1,2},{2,3},{3,0},{4,5},{5,6},{6,7},{7,4},{8,9},{9,10},{10,1... | collective-permute-start | bytes 3145736 | tf_op jit(solution)/shard_map/ppermute | solution.py:398
  192.3 173.8 %collective-permute-start.1 = (bf16[512,1024]{1,0:T(8,128)(2,1)}, bf16[512,1024]{1,0:T(8,128)(2,1)}, u32[]{:S(2)}, u32[]{:S(2)}) collective-permute-start(bf16[512,1024]{1,0:T(8,128)(2,1)} %param.25), channel_id=1, source_target_pairs={{0,2},{1,3},{2,0},{3,1},{4,6},{5,7},{6,4},{7,5},{8,10},{9,11},{10,... | collective-permute-start | bytes 3145736 | tf_op jit(solution)/shard_map/ppermute | solution.py:398
  194.7 173.6 %collective-permute-start.2 = (bf16[512,1024]{1,0:T(8,128)(2,1)}, bf16[512,1024]{1,0:T(8,128)(2,1)}, u32[]{:S(2)}, u32[]{:S(2)}) collective-permute-start(bf16[512,1024]{1,0:T(8,128)(2,1)} %param.25), channel_id=1, source_target_pairs={{0,3},{1,0},{2,1},{3,2},{4,7},{5,4},{6,5},{7,6},{8,11},{9,8},{10,9... | collective-permute-start | bytes 3145736 | tf_op jit(solution)/shard_map/ppermute | solution.py:398
  478.6 92.4 %collective-permute-start.6 = (bf16[512,1024]{1,0:T(8,128)(2,1)}, bf16[512,1024]{1,0:T(8,128)(2,1)}, u32[]{:S(2)}, u32[]{:S(2)}) collective-permute-start(bf16[512,1024]{1,0:T(8,128)(2,1)} %get-tuple-element.119), channel_id=1, source_target_pairs={{0,1},{1,2},{2,3},{3,0},{4,5},{5,6},{6,7},{7,4},{8,9},{9,10},{10,1... | collective-permute-start | bytes 3145736 | tf_op jit(solution)/shard_map/ppermute | solution.py:398
  478.7 92.2 %collective-permute-start.8 = (bf16[512,1024]{1,0:T(8,128)(2,1)}, bf16[512,1024]{1,0:T(8,128)(2,1)}, u32[]{:S(2)}, u32[]{:S(2)}) collective-permute-start(bf16[512,1024]{1,0:T(8,128)(2,1)} %get-tuple-element.120), channel_id=1, source_target_pairs={{0,3},{1,0},{2,1},{3,2},{4,7},{5,4},{6,5},{7,6},{8,11},{9,8},{10,9... | collective-permute-start | bytes 3145736 | tf_op jit(solution)/shard_map/ppermute | solution.py:398
  482.4 88.6 %collective-permute-start.7 = (bf16[512,1024]{1,0:T(8,128)(2,1)}, bf16[512,1024]{1,0:T(8,128)(2,1)}, u32[]{:S(2)}, u32[]{:S(2)}) collective-permute-start(bf16[512,1024]{1,0:T(8,128)(2,1)} %get-tuple-element.121), channel_id=1, source_target_pairs={{0,2},{1,3},{2,0},{3,1},{4,6},{5,7},{6,4},{7,5},{8,10},{9,11},{10,... | collective-permute-start | bytes 3145736 | tf_op jit(solution)/shard_map/ppermute | solution.py:398
  482.4 88.5 %all-to-all-start = ((f32[4,8,512]{2,1,0:T(8,128)}), f32[4,8,512]{2,1,0:T(8,128)S(1)}, u32[]{:S(2)}, u32[]{:S(2)}) async-start(f32[4,8,512]{2,1,0:T(8,128)} %get-tuple-element.40), calls=%async_computation | async-start | bytes 131072 | tf_op jit(solution)/shard_map/all_to_all | solution.py:502
  486.6 269.5 %reduce-scatter.4.cloned.1.call-start = ((), (), s32[]{:S(2)}) async-start(), calls=%async_computation.5 | async-start | bytes 4718592 | tf_op jit(solution)/shard_map/reduce_scatter | solution.py:548
  581.8 22.9 %copy-start.16 = (f32[1,1024]{1,0:T(1,128)S(1)}, f32[1,1024]{1,0:T(1,128)}, u32[]{:S(2)}) copy-start(f32[1,1024]{1,0:T(1,128)} %copy-done.15) | copy-start | bytes 12292
  581.8 22.9 %copy-start.18 = (f32[512]{0:T(512)S(1)}, f32[512]{0:T(512)}, u32[]{:S(2)}) copy-start(f32[512]{0:T(512)} %copy-done.17) | copy-start | bytes 6148
  610.8 145.4 %reduce-scatter.8.cloned.1.call-start = ((), (), s32[]{:S(2)}) async-start(), calls=%async_computation.7 | async-start | bytes 2433024 | tf_op jit(solution)/shard_map/reduce_scatter | solution.py:538
  622.4 179.5 %all-reduce.3.cloned.1.call-start = ((), (), s32[]{:S(2)}) async-start(), calls=%async_computation.10 | async-start | bytes 1589248 | tf_op jit(solution)/shard_map/psum | solution.py:551
  632.1 8.6 %copy-start.23 = (bf16[2,512,1024]{2,1,0:T(8,128)(2,1)S(1)}, bf16[2,512,1024]{2,1,0:T(8,128)(2,1)}, u32[]{:S(2)}) copy-start(bf16[2,512,1024]{2,1,0:T(8,128)(2,1)} %attention_backward.1) | copy-start | bytes 6291460
  636.1 114.4 %collective-permute-start.3 = (bf16[512,1024]{1,0:T(8,128)(2,1)}, bf16[512,1024]{1,0:T(8,128)(2,1)}, u32[]{:S(2)}, u32[]{:S(2)}) collective-permute-start(bf16[512,1024]{1,0:T(8,128)(2,1)} %get-tuple-element.122), channel_id=1, source_target_pairs={{0,1},{1,2},{2,3},{3,0},{4,5},{5,6},{6,7},{7,4},{8,9},{9,10},{10,1... | collective-permute-start | bytes 3145736 | tf_op jit(solution)/shard_map/ppermute | solution.py:398
  637.7 112.8 %collective-permute-start.5 = (bf16[512,1024]{1,0:T(8,128)(2,1)}, bf16[512,1024]{1,0:T(8,128)(2,1)}, u32[]{:S(2)}, u32[]{:S(2)}) collective-permute-start(bf16[512,1024]{1,0:T(8,128)(2,1)} %get-tuple-element.123), channel_id=1, source_target_pairs={{0,3},{1,0},{2,1},{3,2},{4,7},{5,4},{6,5},{7,6},{8,11},{9,8},{10,9... | collective-permute-start | bytes 3145736 | tf_op jit(solution)/shard_map/ppermute | solution.py:398
  639.9 110.6 %collective-permute-start.4 = (bf16[512,1024]{1,0:T(8,128)(2,1)}, bf16[512,1024]{1,0:T(8,128)(2,1)}, u32[]{:S(2)}, u32[]{:S(2)}) collective-permute-start(bf16[512,1024]{1,0:T(8,128)(2,1)} %get-tuple-element.124), channel_id=1, source_target_pairs={{0,2},{1,3},{2,0},{3,1},{4,6},{5,7},{6,4},{7,5},{8,10},{9,11},{10,... | collective-permute-start | bytes 3145736 | tf_op jit(solution)/shard_map/ppermute | solution.py:398
  (17 other events, 48.4 us)
Sparse Core Ops, SparseCore 0:
  13.0 50.4 all-gather.6
  65.3 125.3 all-gather.8
  192.9 149.6 all-gather.10
  463.2 155.9 reduce-scatter.5
  622.4 51.8 reduce-scatter.3
  677.9 41.2 reduce-scatter.7
  756.3 45.5 all-reduce.2
